TPU v7x, 256 devices: a whole 4x4x8 slice. The times are simulated.
256 devices in a mesh: dom: 128 (over y, z, x), slab: 2 (over core).
Axes of the slice: x: 4, y: 4, z: 8, core: 2. Of those that a mesh axis runs over, the one named last changes fastest.
Arguments:
- node_coords: float32 [3, 360448], P(None, ('dom', 'slab')), may hold values from -6 to 6
- displacement: float32 [6, 360448], P(None, ('dom', 'slab')), may hold values from -6 to 6
- stress_operator: bfloat16 [24, 30, 262144], P(None, None, ('dom', 'slab')), may hold values from -1 to 1
- connectivity: int32 [10, 262144], P(None, ('dom', 'slab')), may hold values from 0 to 1791
- node_send: int32 [256, 3, 128], P(('dom', 'slab')), may hold values from 0 to 1407
- element_send: int32 [256, 3, 128], P(('dom', 'slab')), may hold values from 0 to 1023
- patch_elements: int32 [128, 49152], P(None, ('dom', 'slab')), may hold values from 0 to 1407
- patch_count: int32 [256, 192], P(('dom', 'slab')), may hold values from 1 to 128, 8192 in all within a row
Outputs:
- recovered: float32 [12, 49152], P(None, ('dom', 'slab'))
Inputs may be any that keep to these rules, and one draw needn't show every extreme that they name: `patch_elements`: entries at slots beyond a patch's count are arbitrary. `patch_count`: on each partition the 192 counts sum to exactly 8192, and one of them is 128.
All inputs are finite; a program needn't handle non-finite values.
Results may differ from a plain program's by a relative error of at most 0.0003.
Values sent between devices are 32-bit elements; how exact they have to be, the bound alone decides.
No kernel may reach another device: no remote copies, remote signals or barrier semaphores. Data moves between devices by JAX's collectives and lax.ppermute only.
A program may use at most 64 MiB of HBM per device.

v0:
```python
import jax
import jax.numpy as jnp
import numpy as np
from jax import lax
from jax.experimental import pallas as pl
from jax.experimental.pallas import tpu as pltpu
from jax.sharding import PartitionSpec as P

RIDGE = 1.0
LANES = 128
VMEM = pl.BlockSpec(memory_space=pltpu.VMEM)
LIMIT = 24 * 1024 * 1024


def shape_table():
    near = 0.5854101966249685
    far = 0.1381966011250105
    edge_pairs = ((0, 1), (1, 2), (0, 2), (0, 3), (1, 3), (2, 3))
    table_rows = []
    for corner in range(4):
        barycentric = [far, far, far, far]
        barycentric[corner] = near
        values = [b * (2.0 * b - 1.0) for b in barycentric]
        values = values + [4.0 * barycentric[a] * barycentric[b] for a, b in edge_pairs]
        table_rows.append(values)
    return np.array(table_rows, np.float32)


SHAPE = shape_table()


def lane_gather(table, index):
    return jnp.take_along_axis(table, index, axis=1, mode="promise_in_bounds")


def rows8(ref, row, lanes):
    return jnp.broadcast_to(ref[pl.ds(row, 1), lanes], (8, LANES))


def node_pick_kernel(coords_ref, disp_ref, send_ref, prev_ref, next_ref, other_ref, table_ref):
    chunks = coords_ref.shape[1] // LANES
    for chunk in range(chunks):
        lanes = pl.ds(chunk * LANES, LANES)
        table_ref[chunk, 0:3, :] = coords_ref[:, lanes]
        table_ref[chunk, 3:9, :] = disp_ref[:, lanes]
    for side, out_ref in enumerate((prev_ref, next_ref, other_ref)):
        index = jnp.broadcast_to(send_ref[side], (8, LANES))
        low, high = index & 127, index >> 7
        first = jnp.zeros((8, LANES), jnp.float32)
        second = first
        for chunk in range(chunks):
            hit = high == chunk
            first = jnp.where(hit, lane_gather(table_ref[chunk, 0:8, :], low), first)
            second = jnp.where(hit, lane_gather(table_ref[chunk, 8:16, :], low), second)
        out_ref[0:8, :] = first
        out_ref[8:9, :] = second[0:1]


def node_pick(coords, disp, send):
    out = jax.ShapeDtypeStruct((9, LANES), jnp.float32)
    return pl.pallas_call(
        node_pick_kernel,
        out_shape=(out, out, out),
        in_specs=[VMEM] * 3,
        out_specs=(VMEM,) * 3,
        scratch_shapes=[pltpu.VMEM((coords.shape[1] // LANES, 16, LANES), jnp.float32)],
        compiler_params=pltpu.CompilerParams(vmem_limit_bytes=LIMIT),
        name="node_pick",
    )(coords, disp, send)


def own_gather_kernel(coords_ref, disp_ref, conn_ref, out_ref, table_ref):
    chunks = coords_ref.shape[1] // LANES
    for chunk in range(chunks):
        lanes = pl.ds(chunk * LANES, LANES)
        table_ref[chunk, 0:3, :] = coords_ref[:, lanes]
        table_ref[chunk, 3:9, :] = disp_ref[:, lanes]

    def group(block, carry):
        lanes = pl.ds(pl.multiple_of(block * LANES, LANES), LANES)
        for node in range(10):
            index = rows8(conn_ref, node, lanes)
            low, high = index & 127, index >> 7
            first = jnp.zeros((8, LANES), jnp.float32)
            second = first
            for chunk in range(chunks):
                hit = high == chunk
                first = jnp.where(hit, lane_gather(table_ref[chunk, 0:8, :], low), first)
                second = jnp.where(hit, lane_gather(table_ref[chunk, 8:16, :], low), second)
            out_ref[node, 0:8, lanes] = first
            out_ref[node, 8:16, lanes] = second
        return carry

    lax.fori_loop(0, conn_ref.shape[1] // LANES, group, 0)


def own_gather(coords, disp, conn):
    return pl.pallas_call(
        own_gather_kernel,
        out_shape=jax.ShapeDtypeStruct((10, 16, conn.shape[1]), jnp.float32),
        in_specs=[VMEM] * 3,
        out_specs=VMEM,
        scratch_shapes=[pltpu.VMEM((coords.shape[1] // LANES, 16, LANES), jnp.float32)],
        compiler_params=pltpu.CompilerParams(vmem_limit_bytes=LIMIT),
        cost_estimate=pl.CostEstimate(flops=20000000, bytes_accessed=4000000, transcendentals=0),
        name="own_gather",
    )(coords, disp, conn)


def block_kernel(
    first_halo, own_ref, conn_ref, oper_hbm, h0_ref, h1_ref, h2_ref, send_ref,
    blk_ref, prev_ref, next_ref, other_ref, table_ref, full_ref, oper_ref, sem,
):
    copy = pltpu.make_async_copy(oper_hbm, oper_ref, sem)
    copy.start()
    for side, ref in enumerate((h0_ref, h1_ref, h2_ref)):
        table_ref[side, 0:9, :] = ref[...]
    sub = lax.broadcasted_iota(jnp.int32, (8, LANES), 0)
    groups = conn_ref.shape[1] // LANES

    def fill(block, carry):
        lanes = pl.ds(pl.multiple_of(block * LANES, LANES), LANES)
        for node in range(10):
            index = rows8(conn_ref, node, lanes)
            low, high = index & 127, index >> 7
            first = own_ref[node, 0:8, lanes]
            second = own_ref[node, 8:16, lanes]
            for side in range(3):
                hit = high == first_halo + side
                first = jnp.where(hit, lane_gather(table_ref[side, 0:8, :], low), first)
                second = jnp.where(hit, lane_gather(table_ref[side, 8:16, :], low), second)
            full_ref[node, 0:8, lanes] = first
            full_ref[node, 8:16, lanes] = second
        return carry

    lax.fori_loop(0, groups, fill, 0)
    copy.wait()

    def stress(block, carry):
        lanes = pl.ds(pl.multiple_of(block * LANES, LANES), LANES)
        totals = [jnp.zeros((24, LANES), jnp.float32) for _ in range(2)]
        for node in range(10):
            for comp in range(3):
                oper = oper_ref[3 * node + comp, :, lanes].astype(jnp.float32)
                for step in range(2):
                    value = full_ref[node, pl.ds(3 + 3 * step + comp, 1), lanes]
                    totals[step] = totals[step] + oper * value
        blk_ref[0:24, lanes] = totals[0]
        blk_ref[24:48, lanes] = totals[1]
        nodes = [full_ref[node, 0:8, lanes] for node in range(10)]
        points = []
        for quad in range(4):
            total = nodes[0] * SHAPE[quad, 0]
            for node in range(1, 10):
                total = total + nodes[node] * SHAPE[quad, node]
            points.append(total)
        blk_ref[48:56, lanes] = jnp.where(sub < 4, points[0], pltpu.roll(points[1], 4, 0))
        blk_ref[56:64, lanes] = jnp.where(sub < 4, points[2], pltpu.roll(points[3], 4, 0))
        return carry

    lax.fori_loop(0, groups, stress, 0)
    for side, out_ref in enumerate((prev_ref, next_ref, other_ref)):
        index = jnp.broadcast_to(send_ref[side], (8, LANES))
        low, high = index & 127, index >> 7
        hits = [high == chunk for chunk in range(groups)]
        for row in range(0, 64, 8):
            total = jnp.zeros((8, LANES), jnp.float32)
            for chunk in range(groups):
                piece = blk_ref[row:row + 8, chunk * LANES:(chunk + 1) * LANES]
                total = jnp.where(hits[chunk], lane_gather(piece, low), total)
            out_ref[row:row + 8, :] = total


def make_blocks(own, conn, oper, halos, send, first_halo):
    elems = conn.shape[1]
    out = jax.ShapeDtypeStruct((64, LANES), jnp.float32)

    def kernel(*refs):
        block_kernel(first_halo, *refs)

    return pl.pallas_call(
        kernel,
        out_shape=(jax.ShapeDtypeStruct((64, elems), jnp.float32), out, out, out),
        in_specs=[VMEM, VMEM, pl.BlockSpec(memory_space=pl.ANY)] + [VMEM] * 4,
        out_specs=(VMEM,) * 4,
        scratch_shapes=[
            pltpu.VMEM((3, 16, LANES), jnp.float32),
            pltpu.VMEM((10, 16, elems), jnp.float32),
            pltpu.VMEM(oper.shape, oper.dtype),
            pltpu.SemaphoreType.DMA,
        ],
        compiler_params=pltpu.CompilerParams(vmem_limit_bytes=LIMIT),
        name="make_blocks",
    )(own, conn, oper, *halos, send)


def add_points(sub, piece):
    pair = jnp.where(sub >= 6, piece[0], piece[1])
    later = jnp.where(sub >= 4, piece[1], piece[2])
    return piece[0] + pltpu.roll(pair, 2, 0) + pltpu.roll(later, 4, 0) + pltpu.roll(piece[2], 6, 0)


def moment_rows(sub, ref, lanes, out_ref, out_lanes):
    spread = []
    for dim in range(3):
        rows = [rows8(ref, 48 + 4 * quad + dim, lanes) for quad in range(4)]
        spread.append([jnp.where(sub < 6 - 2 * k, rows[k], rows[k + 1]) for k in range(3)])
    for step in range(2):
        piece = [ref[24 * step + 8 * k:24 * step + 8 * k + 8, lanes] for k in range(3)]
        base = 32 * step
        out_ref[base:base + 8, out_lanes] = add_points(sub, piece)
        for dim in range(3):
            scaled = [piece[k] * spread[dim][k] for k in range(3)]
            out_ref[base + 8 * dim + 8:base + 8 * dim + 16, out_lanes] = add_points(sub, scaled)
    pair = [ref[48:56, lanes], ref[56:64, lanes]]
    out_ref[64:72, out_lanes] = pair[0] + pair[1]
    out_ref[72:80, out_lanes] = pair[0] * pair[0] + pair[1] * pair[1]
    for shift in (1, 2):
        total = pair[0] * pltpu.roll(pair[0], 8 - shift, 0) + pair[1] * pltpu.roll(pair[1], 8 - shift, 0)
        out_ref[72 + 8 * shift:80 + 8 * shift, out_lanes] = total


def summed_over(moments, weights):
    total = None
    rest = moments
    for part in range(3):
        piece = rest.astype(jnp.bfloat16)
        if part < 2:
            rest = rest - piece.astype(jnp.float32)
        term = lax.dot_general(
            piece, weights, (((1,), (1,)), ((), ())), preferred_element_type=jnp.float32
        )
        total = term if total is None else total + term
    return total


def weight_kernel(list_ref, count_ref, weight_ref, index_ref, hist_ref):
    patches, slots = list_ref.shape
    counts = count_ref[...].astype(jnp.float32)
    diagonal = lax.broadcasted_iota(jnp.int32, (patches, patches), 0) == lax.broadcasted_iota(
        jnp.int32, (patches, patches), 1
    )
    spread = jnp.where(diagonal, jnp.broadcast_to(counts, (patches, patches)), 0.0)
    limits = jnp.dot(
        spread.astype(jnp.bfloat16),
        jnp.ones((patches, slots), jnp.bfloat16),
        preferred_element_type=jnp.float32,
    ).astype(jnp.int32)
    slot = lax.broadcasted_iota(jnp.int32, (patches, slots), 1)
    index_ref[...] = jnp.where(slot < limits, list_ref[...], 4095)
    low_ids = lax.broadcasted_iota(jnp.int32, (LANES, slots), 0)
    high_ids = lax.broadcasted_iota(jnp.int32, (16, slots), 0)
    width = 8

    def group(block, carry):
        start = pl.multiple_of(block * width, width)
        listed = index_ref[pl.ds(start, width), :]
        low, high = listed & 127, listed >> 7
        for patch in range(width):
            low_hit = low_ids == jnp.broadcast_to(low[patch:patch + 1], (LANES, slots))
            high_hit = high_ids == jnp.broadcast_to(high[patch:patch + 1], (16, slots))
            hist = lax.dot_general(
                jnp.where(high_hit, 1.0, 0.0).astype(jnp.bfloat16),
                jnp.where(low_hit, 1.0, 0.0).astype(jnp.bfloat16),
                (((1,), (1,)), ((), ())),
                preferred_element_type=jnp.float32,
            )
            hist_ref[pl.ds(pl.multiple_of(start * 16, LANES) + 16 * patch, 16), :] = hist
        return carry

    lax.fori_loop(0, patches // width, group, 0)
    for chunk in range(weight_ref.shape[1] // LANES):
        column = hist_ref[pl.ds(chunk, patches, stride=16), :]
        weight_ref[:, chunk * LANES:(chunk + 1) * LANES] = column.astype(jnp.bfloat16)


def make_weights(listed, counts, width):
    patches, slots = listed.shape
    return pl.pallas_call(
        weight_kernel,
        out_shape=jax.ShapeDtypeStruct((patches, width), jnp.bfloat16),
        in_specs=[VMEM] * 2,
        out_specs=VMEM,
        scratch_shapes=[
            pltpu.VMEM((patches, slots), jnp.int32),
            pltpu.VMEM((patches * 16, LANES), jnp.float32),
        ],
        compiler_params=pltpu.CompilerParams(vmem_limit_bytes=LIMIT),
        cost_estimate=pl.CostEstimate(flops=20000000, bytes_accessed=8000000, transcendentals=0),
        name="make_weights",
    )(listed, counts)


def own_sum_kernel(blk_ref, weight_ref, sum_ref, moment_ref):
    sub = lax.broadcasted_iota(jnp.int32, (8, LANES), 0)
    elems = blk_ref.shape[1]

    def group(block, carry):
        lanes = pl.ds(pl.multiple_of(block * LANES, LANES), LANES)
        moment_rows(sub, blk_ref, lanes, moment_ref, lanes)
        return carry

    lax.fori_loop(0, elems // LANES, group, 0)
    sum_ref[...] = summed_over(moment_ref[...], weight_ref[:, 0:elems])


def own_sums(blk, weights):
    return pl.pallas_call(
        own_sum_kernel,
        out_shape=jax.ShapeDtypeStruct((96, weights.shape[0]), jnp.float32),
        in_specs=[VMEM] * 2,
        out_specs=VMEM,
        scratch_shapes=[pltpu.VMEM((96, blk.shape[1]), jnp.float32)],
        compiler_params=pltpu.CompilerParams(vmem_limit_bytes=LIMIT),
        cost_estimate=pl.CostEstimate(flops=20000000, bytes_accessed=4000000, transcendentals=0),
        name="own_sums",
    )(blk, weights)


def fit_kernel(sum_ref, weight_ref, h0_ref, h1_ref, h2_ref, vertex_ref, count_ref, out_ref, moment_ref, total_ref):
    sub = lax.broadcasted_iota(jnp.int32, (8, LANES), 0)
    for side, ref in enumerate((h0_ref, h1_ref, h2_ref)):
        moment_rows(sub, ref, slice(0, LANES), moment_ref, slice(side * LANES, (side + 1) * LANES))
    width = moment_ref.shape[1]
    own = weight_ref.shape[1] - width
    patches = weight_ref.shape[0]
    total_ref[...] = sum_ref[...] + summed_over(moment_ref[...], weight_ref[:, own:own + width])

    def row(ref, start):
        return jnp.broadcast_to(ref[start:start + 1, 0:patches], (8, patches))

    def both(start):
        return row(total_ref, start) + row(total_ref, start + 4)

    points = 4.0 * row(count_ref, 0).astype(jnp.float32)
    vertex = [row(vertex_ref, dim) for dim in range(3)]
    sum_x = [both(64 + dim) for dim in range(3)]
    sum_xx = {
        (0, 0): both(72), (1, 1): both(73), (2, 2): both(74),
        (0, 1): both(80), (1, 2): both(81), (0, 2): both(88),
    }
    gram = {(0, 0): points + RIDGE}
    for a in range(3):
        gram[0, a + 1] = sum_x[a] - points * vertex[a]
        for b in range(a, 3):
            value = sum_xx[a, b] - vertex[a] * sum_x[b] - sum_x[a] * vertex[b] + points * vertex[a] * vertex[b]
            gram[a + 1, b + 1] = value + RIDGE if a == b else value
    rhs = []
    for step in range(2):
        base = total_ref[32 * step:32 * step + 8, :]
        rest = [total_ref[32 * step + 8 * dim + 8:32 * step + 8 * dim + 16, :] for dim in range(3)]
        rhs.append([base] + [rest[dim] - vertex[dim] * base for dim in range(3)])
    for pivot in (3, 2, 1):
        inverse = 1.0 / gram[pivot, pivot]
        for other in range(pivot):
            factor = gram[other, pivot] * inverse
            for column in range(other, pivot):
                gram[other, column] = gram[other, column] - factor * gram[column, pivot]
            for step in range(2):
                rhs[step][other] = rhs[step][other] - factor * rhs[step][pivot]
    inverse = 1.0 / gram[0, 0]
    for step in range(2):
        out_ref[6 * step:6 * step + 6, :] = (rhs[step][0] * inverse)[0:6]


def fit(sums, weights, halos, coords, counts):
    patches = weights.shape[0]
    return pl.pallas_call(
        fit_kernel,
        out_shape=jax.ShapeDtypeStruct((12, patches), jnp.float32),
        in_specs=[VMEM] * 7,
        out_specs=VMEM,
        scratch_shapes=[
            pltpu.VMEM((96, 3 * LANES), jnp.float32),
            pltpu.VMEM((96, patches), jnp.float32),
        ],
        compiler_params=pltpu.CompilerParams(vmem_limit_bytes=LIMIT),
        name="fit",
    )(sums, weights, *halos, coords, counts)


def exchange(to_prev, to_next, to_other):
    count = lax.axis_size("dom")
    up = [(i, (i + 1) % count) for i in range(count)]
    down = [(j, i) for i, j in up]
    swap = [(0, 1), (1, 0)]
    from_prev = lax.ppermute(to_next, "dom", up)
    from_next = lax.ppermute(to_prev, "dom", down)
    from_other = lax.ppermute(to_other, "slab", swap)
    return from_prev, from_next, from_other


def local(coords, disp, oper, conn, node_send, element_send, patch_elements, patch_count):
    node_send = node_send.transpose(1, 0, 2)
    element_send = element_send.transpose(1, 0, 2)
    oper = oper.transpose(1, 0, 2)
    listed = patch_elements.T
    picked = node_pick(coords, disp, node_send)
    halos = exchange(*picked)
    own = own_gather(coords, disp, conn)
    blk, *picked = make_blocks(own, conn, oper, halos, element_send, coords.shape[1] // LANES)
    weights = make_weights(listed, patch_count, conn.shape[1] + 3 * LANES)
    halos = exchange(*picked)
    sums = own_sums(blk, weights)
    return fit(sums, weights, halos, coords, patch_count)


def solution(mesh):
    both = ("dom", "slab")
    in_specs = (
        P(None, both),
        P(None, both),
        P(None, None, both),
        P(None, both),
        P(both, None, None),
        P(both, None, None),
        P(None, both),
        P(both, None),
    )
    return jax.shard_map(local, mesh=mesh, in_specs=in_specs, out_specs=P(None, both), check_vma=False)
```

profile of v0, /device:TPU:1, one launch (start us, length us, event | category | flops | bytes accessed | tf_op | source)
XLA Modules:
  0.0 39.9 jit_solution(14401802548225610006)
XLA Ops:
  0.0 0.0 copy-start.3
  0.0 0.7 %copy-done.3 = f32[3,1408]{1,0:T(4,128)S(1)} copy-done((f32[3,1408]{1,0:T(4,128)S(1)}, f32[3,1408]{1,0:T(4,128)}, u32[]{:S(2)}) %copy-start.3) | copy-done | bytes 16920
  0.7 0.0 copy-start.5
  0.7 0.8 %copy-done.5 = f32[6,1408]{1,0:T(8,128)S(1)} copy-done((f32[6,1408]{1,0:T(8,128)S(1)}, f32[6,1408]{1,0:T(8,128)}, u32[]{:S(2)}) %copy-start.5) | copy-done | bytes 33816
  1.5 0.0 copy-start.9
  1.5 0.7 %copy-done.9 = s32[1,3,128]{2,0,1:T(1,128)S(1)} copy-done((s32[1,3,128]{2,0,1:T(1,128)S(1)}, s32[1,3,128]{2,0,1:T(1,128)}, u32[]{:S(2)}) %copy-start.9) | copy-done | bytes 1560
  2.2 0.1 node_pick.1
  2.4 2.1 %collective-permute-start = (f32[9,128]{1,0:T(8,128)S(1)}, f32[9,128]{1,0:T(8,128)S(1)}, u32[]{:S(2)}, u32[]{:S(2)}) collective-permute-start(f32[9,128]{1,0:T(8,128)S(1)} %get-tuple-element.12), channel_id=1, source_target_pairs={{0,2},{2,4},{4,6},{6,8},{8,10},{10,12},{12,14},{14,16},{16,18},{18... | collective-permute-start | bytes 13832 | tf_op jit(solution)/shard_map/ppermute | solution.py:387
  4.5 9.1 %collective-permute-start.1 = (f32[9,128]{1,0:T(8,128)S(1)}, f32[9,128]{1,0:T(8,128)S(1)}, u32[]{:S(2)}, u32[]{:S(2)}) collective-permute-start(f32[9,128]{1,0:T(8,128)S(1)} %get-tuple-element.13), channel_id=1, source_target_pairs={{2,0},{4,2},{6,4},{8,6},{10,8},{12,10},{14,12},{16,14},{18,16},{20... | collective-permute-start | bytes 13832 | tf_op jit(solution)/shard_map/ppermute | solution.py:388
  13.6 1.0 %collective-permute-start.2 = (f32[9,128]{1,0:T(8,128)S(1)}, f32[9,128]{1,0:T(8,128)S(1)}, u32[]{:S(2)}, u32[]{:S(2)}) collective-permute-start(f32[9,128]{1,0:T(8,128)S(1)} %get-tuple-element.14), channel_id=1, source_target_pairs={{0,1},{1,0},{2,3},{3,2},{4,5},{5,4},{6,7},{7,6},{8,9},{9,8},{10,11... | collective-permute-start | bytes 13832 | tf_op jit(solution)/shard_map/ppermute | solution.py:389
  14.5 0.0 copy-start.1
  14.5 0.8 %copy-done.1 = s32[10,1024]{1,0:T(8,128)S(1)} copy-done((s32[10,1024]{1,0:T(8,128)S(1)}, s32[10,1024]{1,0:T(8,128)}, u32[]{:S(2)}) %copy-start.1) | copy-done | bytes 40984
  15.4 0.0 copy-start.6
  15.4 0.0 copy-start.7
  15.4 2.7 %own_gather.1.refs_0_ = f32[10,16,1024]{2,1,0:T(8,128)S(1)} custom-call(f32[3,1408]{1,0:T(4,128)S(1)} %copy-done.3, f32[6,1408]{1,0:T(8,128)S(1)} %copy-done.5, s32[10,1024]{1,0:T(8,128)S(1)} %copy-done.1), custom_call_target="tpu_custom_call" | custom-call | flops 20000000 | bytes 4000000 | tf_op jit(solution)/shard_map/own_gather/pallas_call | solution.py:98
  18.0 0.0 collective-permute-done.refs_3_
  18.1 0.0 collective-permute-done.1.refs_4_
  18.1 0.0 collective-permute-done.2.refs_5_
  18.1 0.0 copy-start
  18.1 1.4 %copy-done = bf16[24,30,1024]{2,0,1:T(8,128)(2,1)S(1)} copy-done((bf16[24,30,1024]{2,0,1:T(8,128)(2,1)S(1)}, bf16[24,30,1024]{2,0,1:T(8,128)(2,1)}, u32[]{:S(2)}) %copy-start) | copy-done | bytes 1474584
  19.5 0.0 copy-start.2
  19.5 0.8 %copy-done.2 = s32[10,1024]{1,0:T(8,128)S(1)} copy-done((s32[10,1024]{1,0:T(8,128)S(1)}, s32[10,1024]{1,0:T(8,128)}, u32[]{:S(2)}) %copy-start.2) | copy-done | bytes 40984
  20.3 0.0 copy-start.8
  20.3 0.7 %copy-done.8 = s32[1,3,128]{2,0,1:T(1,128)S(1)} copy-done((s32[1,3,128]{2,0,1:T(1,128)S(1)}, s32[1,3,128]{2,0,1:T(1,128)}, u32[]{:S(2)}) %copy-start.8) | copy-done | bytes 1560
  21.0 0.0 copy-start.4
  21.0 2.9 %make_blocks.1 = (f32[64,1024]{1,0:T(8,128)S(1)}, f32[64,128]{1,0:T(8,128)S(1)}, f32[64,128]{1,0:T(8,128)S(1)}, f32[64,128]{1,0:T(8,128)S(1)}) custom-call(f32[10,16,1024]{2,1,0:T(8,128)S(1)} %own_gather.1.refs_0_, s32[10,1024]{1,0:T(8,128)S(1)} %copy-done.2, bf16[30,24,1024]{2,1,0:T(8,128)(2,1)S(1)} %bitcast.4, f32[9,128]{1,0:T(8,128)S(1)} %collective-permute-done.refs_3_, ...), custom_call_target="tpu_custom_call" | custom-call | tf_op jit(solution)/shard_map/make_blocks/pallas_call | solution.py:181
  23.9 0.1 collective-permute-start.3
  24.0 6.9 %collective-permute-start.4 = (f32[64,128]{1,0:T(8,128)S(1)}, f32[64,128]{1,0:T(8,128)S(1)}, u32[]{:S(2)}, u32[]{:S(2)}) collective-permute-start(f32[64,128]{1,0:T(8,128)S(1)} %get-tuple-element.17), channel_id=1, source_target_pairs={{2,0},{4,2},{6,4},{8,6},{10,8},{12,10},{14,12},{16,14},{18,16},{20... | collective-permute-start | bytes 98312 | tf_op jit(solution)/shard_map/ppermute | solution.py:388
  30.9 0.6 %collective-permute-start.5 = (f32[64,128]{1,0:T(8,128)S(1)}, f32[64,128]{1,0:T(8,128)S(1)}, u32[]{:S(2)}, u32[]{:S(2)}) collective-permute-start(f32[64,128]{1,0:T(8,128)S(1)} %get-tuple-element.18), channel_id=1, source_target_pairs={{0,1},{1,0},{2,3},{3,2},{4,5},{5,4},{6,7},{7,6},{8,9},{9,8},{10,11... | collective-permute-start | bytes 98312 | tf_op jit(solution)/shard_map/ppermute | solution.py:389
  31.4 0.0 copy-done.6
  31.4 0.0 copy-done.7
  31.4 6.7 %make_weights.1.weight_ref = bf16[192,1408]{1,0:T(8,128)(2,1)S(1)} custom-call(s32[192,128]{1,0:T(8,128)S(1)} %bitcast.5, s32[1,192]{1,0:T(1,128)S(1)} %copy-done.7), custom_call_target="tpu_custom_call" | custom-call | flops 20000000 | bytes 8000000 | tf_op jit(solution)/shard_map/make_weights/pallas_call | solution.py:279
  38.2 0.7 %own_sums.1.sum_ref = f32[96,192]{1,0:T(8,128)S(1)} custom-call(f32[64,1024]{1,0:T(8,128)S(1)} %get-tuple-element.15.blk_ref, bf16[192,1408]{1,0:T(8,128)(2,1)S(1)} %make_weights.1.weight_ref), custom_call_target="tpu_custom_call" | custom-call | flops 20000000 | bytes 4000000 | tf_op jit(solution)/shard_map/own_sums/pallas_call | solution.py:308
  38.8 0.0 collective-permute-done.3.h0_ref
  38.8 0.0 collective-permute-done.4.h1_ref
  38.9 0.0 collective-permute-done.5.h2_ref
  38.9 0.0 copy-done.4
  38.9 1.0 %fit.1 = f32[12,192]{1,0:T(8,128)} custom-call(f32[96,192]{1,0:T(8,128)S(1)} %own_sums.1.sum_ref, bf16[192,1408]{1,0:T(8,128)(2,1)S(1)} %make_weights.1.weight_ref, f32[64,128]{1,0:T(8,128)S(1)} %collective-permute-done.3.h0_ref, f32[64,128]{1,0:T(8,128)S(1)} %collective-permute-done.4.h1_ref, f32[64,128]{1,0:T(8,128)S(1)} %collective-permute-done.5.h2_ref, ...), custom_call_target="tpu_custom_call" | custom-call | tf_op jit(solution)/shard_map/fit/pallas_call | solution.py:368
Async XLA Ops:
  0.0 0.7 %copy-start.3 = (f32[3,1408]{1,0:T(4,128)S(1)}, f32[3,1408]{1,0:T(4,128)}, u32[]{:S(2)}) copy-start(f32[3,1408]{1,0:T(4,128)} %vertex_ref.1) | copy-start | bytes 50692
  0.7 0.8 %copy-start.5 = (f32[6,1408]{1,0:T(8,128)S(1)}, f32[6,1408]{1,0:T(8,128)}, u32[]{:S(2)}) copy-start(f32[6,1408]{1,0:T(8,128)} %disp_ref.3) | copy-start | bytes 101380
  1.5 0.7 %copy-start.9 = (s32[1,3,128]{2,0,1:T(1,128)S(1)}, s32[1,3,128]{2,0,1:T(1,128)}, u32[]{:S(2)}) copy-start(s32[1,3,128]{2,0,1:T(1,128)} %param.12) | copy-start | bytes 4612
  2.4 15.7 %collective-permute-start = (f32[9,128]{1,0:T(8,128)S(1)}, f32[9,128]{1,0:T(8,128)S(1)}, u32[]{:S(2)}, u32[]{:S(2)}) collective-permute-start(f32[9,128]{1,0:T(8,128)S(1)} %get-tuple-element.12), channel_id=1, source_target_pairs={{0,2},{2,4},{4,6},{6,8},{8,10},{10,12},{12,14},{14,16},{16,18},{18... | collective-permute-start | bytes 13832 | tf_op jit(solution)/shard_map/ppermute | solution.py:387
  4.5 13.6 %collective-permute-start.1 = (f32[9,128]{1,0:T(8,128)S(1)}, f32[9,128]{1,0:T(8,128)S(1)}, u32[]{:S(2)}, u32[]{:S(2)}) collective-permute-start(f32[9,128]{1,0:T(8,128)S(1)} %get-tuple-element.13), channel_id=1, source_target_pairs={{2,0},{4,2},{6,4},{8,6},{10,8},{12,10},{14,12},{16,14},{18,16},{20... | collective-permute-start | bytes 13832 | tf_op jit(solution)/shard_map/ppermute | solution.py:388
  13.6 4.5 %collective-permute-start.2 = (f32[9,128]{1,0:T(8,128)S(1)}, f32[9,128]{1,0:T(8,128)S(1)}, u32[]{:S(2)}, u32[]{:S(2)}) collective-permute-start(f32[9,128]{1,0:T(8,128)S(1)} %get-tuple-element.14), channel_id=1, source_target_pairs={{0,1},{1,0},{2,3},{3,2},{4,5},{5,4},{6,7},{7,6},{8,9},{9,8},{10,11... | collective-permute-start | bytes 13832 | tf_op jit(solution)/shard_map/ppermute | solution.py:389
  14.5 0.8 %copy-start.1 = (s32[10,1024]{1,0:T(8,128)S(1)}, s32[10,1024]{1,0:T(8,128)}, u32[]{:S(2)}) copy-start(s32[10,1024]{1,0:T(8,128)} %refs_1_.1) | copy-start | bytes 122884
  15.4 16.1 %copy-start.6 = (s32[128,192]{0,1:T(8,128)S(1)}, s32[128,192]{0,1:T(8,128)}, u32[]{:S(2)}) copy-start(s32[128,192]{0,1:T(8,128)} %param.14) | copy-start | bytes 294916
  15.4 16.1 %copy-start.7 = (s32[1,192]{1,0:T(1,128)S(1)}, s32[1,192]{1,0:T(1,128)}, u32[]{:S(2)}) copy-start(s32[1,192]{1,0:T(1,128)} %count_ref.3) | copy-start | bytes 2308
  18.1 1.4 %copy-start = (bf16[24,30,1024]{2,0,1:T(8,128)(2,1)S(1)}, bf16[24,30,1024]{2,0,1:T(8,128)(2,1)}, u32[]{:S(2)}) copy-start(bf16[24,30,1024]{2,0,1:T(8,128)(2,1)} %param.10) | copy-start | bytes 4423684
  19.5 0.8 %copy-start.2 = (s32[10,1024]{1,0:T(8,128)S(1)}, s32[10,1024]{1,0:T(8,128)}, u32[]{:S(2)}) copy-start(s32[10,1024]{1,0:T(8,128)} %refs_1_.1) | copy-start | bytes 122884
  20.3 0.7 %copy-start.8 = (s32[1,3,128]{2,0,1:T(1,128)S(1)}, s32[1,3,128]{2,0,1:T(1,128)}, u32[]{:S(2)}) copy-start(s32[1,3,128]{2,0,1:T(1,128)} %param.13) | copy-start | bytes 4612
  21.0 17.9 %copy-start.4 = (f32[3,1408]{1,0:T(4,128)S(1)}, f32[3,1408]{1,0:T(4,128)}, u32[]{:S(2)}) copy-start(f32[3,1408]{1,0:T(4,128)} %vertex_ref.1) | copy-start | bytes 50692
  23.9 15.0 %collective-permute-start.3 = (f32[64,128]{1,0:T(8,128)S(1)}, f32[64,128]{1,0:T(8,128)S(1)}, u32[]{:S(2)}, u32[]{:S(2)}) collective-permute-start(f32[64,128]{1,0:T(8,128)S(1)} %get-tuple-element.16), channel_id=1, source_target_pairs={{0,2},{2,4},{4,6},{6,8},{8,10},{10,12},{12,14},{14,16},{16,18},{18... | collective-permute-start | bytes 98312 | tf_op jit(solution)/shard_map/ppermute | solution.py:387
  24.0 14.9 %collective-permute-start.4 = (f32[64,128]{1,0:T(8,128)S(1)}, f32[64,128]{1,0:T(8,128)S(1)}, u32[]{:S(2)}, u32[]{:S(2)}) collective-permute-start(f32[64,128]{1,0:T(8,128)S(1)} %get-tuple-element.17), channel_id=1, source_target_pairs={{2,0},{4,2},{6,4},{8,6},{10,8},{12,10},{14,12},{16,14},{18,16},{20... | collective-permute-start | bytes 98312 | tf_op jit(solution)/shard_map/ppermute | solution.py:388
  30.9 8.0 %collective-permute-start.5 = (f32[64,128]{1,0:T(8,128)S(1)}, f32[64,128]{1,0:T(8,128)S(1)}, u32[]{:S(2)}, u32[]{:S(2)}) collective-permute-start(f32[64,128]{1,0:T(8,128)S(1)} %get-tuple-element.18), channel_id=1, source_target_pairs={{0,1},{1,0},{2,3},{3,2},{4,5},{5,4},{6,7},{7,6},{8,9},{9,8},{10,11... | collective-permute-start | bytes 98312 | tf_op jit(solution)/shard_map/ppermute | solution.py:389
where the time goes:
time: 40.2 us; the launch traced here: 39.9 us
  starting transfers between devices  19.7 us (49%)
  Pallas kernels  14.1 us (35%)
  local copies, waits for them, and re-layouts  5.94 us (15%)
    ppermute x2, starting transfers between devices, exchange(): from_next = lax.ppermute(to_prev, 'dom', down)  16 us
    pallas_call x1, Pallas kernels, make_weights(): pl.pallas_call(weight_kernel, out_shape=jax.ShapeDtypeStruct((patches, wi...  6.73 us
    unnamed x20, local copies, waits for them, and re-layouts  5.94 us
    pallas_call x1, Pallas kernels, make_blocks(): pl.pallas_call(kernel, out_shape=(jax.ShapeDtypeStruct((64, elems), jnp.f...  2.9 us
    pallas_call x1, Pallas kernels, own_gather(): pl.pallas_call(own_gather_kernel, out_shape=jax.ShapeDtypeStruct((10, 16,...  2.67 us
    ppermute x2, starting transfers between devices, exchange(): from_prev = lax.ppermute(to_next, 'dom', up)  2.2 us
    ppermute x2, starting transfers between devices, exchange(): from_other = lax.ppermute(to_other, 'slab', swap)  1.52 us
    pallas_call x1, Pallas kernels, fit(): pl.pallas_call(fit_kernel, out_shape=jax.ShapeDtypeStruct((12, patches),...  0.98 us
  transfers between devices with their start and end apart: 6, of which 0 were waited for; matrix products, arithmetic and copies ran while one was open for 0% of the time, Pallas kernels for 25%

commit v1 on v0

v1 whole, which is shorter than its diff:
```python
import jax
import jax.numpy as jnp
import numpy as np
from jax import lax
from jax.experimental import pallas as pl
from jax.experimental.pallas import tpu as pltpu
from jax.sharding import PartitionSpec as P

RIDGE = 1.0
LANES = 128
VMEM = pl.BlockSpec(memory_space=pltpu.VMEM)
HBM = pl.BlockSpec(memory_space=pltpu.HBM)
UNROLL = 2
WIDTH = 64
LIMIT = 24 * 1024 * 1024


def shape_table():
    near = 0.5854101966249685
    far = 0.1381966011250105
    edge_pairs = ((0, 1), (1, 2), (0, 2), (0, 3), (1, 3), (2, 3))
    table_rows = []
    for corner in range(4):
        barycentric = [far, far, far, far]
        barycentric[corner] = near
        values = [b * (2.0 * b - 1.0) for b in barycentric]
        values = values + [4.0 * barycentric[a] * barycentric[b] for a, b in edge_pairs]
        table_rows.append(values)
    return np.array(table_rows, np.float32)


SHAPE = shape_table()


def lane_gather(table, index):
    return jnp.take_along_axis(table, index, axis=1, mode="promise_in_bounds")


def rows8(ref, row, lanes):
    return jnp.broadcast_to(ref[pl.ds(row, 1), lanes], (8, LANES))


def start_all(pairs, sems):
    copies = [pltpu.make_async_copy(src, dst, sems.at[k]) for k, (src, dst) in enumerate(pairs)]
    for copy in copies:
        copy.start()
    return copies


def ninth_row(sub, table, low, high, chunks):
    total = jnp.zeros((8, LANES), jnp.float32)
    for start in range(0, chunks, 8):
        piece = lane_gather(table[start:start + 8, :], low)
        total = jnp.where(high == sub + start, piece, total)
    return total


def node_pick_kernel(
    coords_hbm, disp_hbm, send_hbm, conn_hbm,
    prev_ref, next_ref, other_ref, table_ref, ninth_ref, coords_ref, conn_ref,
    disp_ref, send_ref, sems,
):
    pairs = ((coords_hbm, coords_ref), (disp_hbm, disp_ref), (send_hbm, send_ref), (conn_hbm, conn_ref))
    copies = start_all(pairs, sems)
    for copy in copies[0:3]:
        copy.wait()
    sub = lax.broadcasted_iota(jnp.int32, (8, LANES), 0)
    chunks = table_ref.shape[0]
    ninth_ref[8:16, :] = jnp.zeros((8, LANES), jnp.float32)
    for chunk in range(chunks):
        lanes = pl.ds(chunk * LANES, LANES)
        table_ref[chunk, 0:3, :] = coords_ref[:, lanes]
        table_ref[chunk, 3:8, :] = disp_ref[0:5, lanes]
        ninth_ref[chunk:chunk + 1, :] = disp_ref[5:6, lanes]
    for side, out_ref in enumerate((prev_ref, next_ref, other_ref)):
        index = jnp.broadcast_to(send_ref[side], (8, LANES))
        low, high = index & 127, index >> 7
        first = jnp.zeros((8, LANES), jnp.float32)
        for chunk in range(chunks):
            first = jnp.where(high == chunk, lane_gather(table_ref[chunk], low), first)
        out_ref[0:8, :] = first
        last = ninth_row(sub, ninth_ref, low, high, chunks)
        out_ref[8:9, :] = jnp.sum(last, axis=0, keepdims=True)
    copies[3].wait()


def node_pick(coords, disp, send, conn):
    out = jax.ShapeDtypeStruct((9, LANES), jnp.float32)
    chunks = coords.shape[1] // LANES
    return pl.pallas_call(
        node_pick_kernel,
        out_shape=(
            out, out, out,
            jax.ShapeDtypeStruct((chunks, 8, LANES), jnp.float32),
            jax.ShapeDtypeStruct((16, LANES), jnp.float32),
            jax.ShapeDtypeStruct(coords.shape, coords.dtype),
            jax.ShapeDtypeStruct(conn.shape, conn.dtype),
        ),
        in_specs=[HBM] * 4,
        out_specs=(VMEM,) * 7,
        scratch_shapes=[
            pltpu.VMEM(disp.shape, disp.dtype),
            pltpu.VMEM(send.shape, send.dtype),
            pltpu.SemaphoreType.DMA((4,)),
        ],
        compiler_params=pltpu.CompilerParams(vmem_limit_bytes=LIMIT),
        name="node_pick",
    )(coords, disp, send, conn)


def own_gather_kernel(
    table_ref, ninth_ref, conn_ref, oper_hbm, list_hbm, count_hbm, send_hbm,
    first_ref, last_ref, oper_ref, list_ref, count_ref, send_ref, sems,
):
    pairs = ((oper_hbm, oper_ref), (list_hbm, list_ref), (count_hbm, count_ref), (send_hbm, send_ref))
    copies = start_all(pairs, sems)
    sub = lax.broadcasted_iota(jnp.int32, (8, LANES), 0)
    chunks = table_ref.shape[0]

    def group(block, carry):
        lanes = pl.ds(pl.multiple_of(block * LANES, LANES), LANES)
        for node in range(10):
            index = rows8(conn_ref, node, lanes)
            low, high = index & 127, index >> 7
            first = jnp.zeros((8, LANES), jnp.float32)
            for chunk in range(chunks):
                first = jnp.where(high == chunk, lane_gather(table_ref[chunk], low), first)
            first_ref[node, :, lanes] = first
            last = ninth_row(sub, ninth_ref, low, high, chunks)
            last_ref[node:node + 1, lanes] = jnp.sum(last, axis=0, keepdims=True)
        return carry

    lax.fori_loop(0, conn_ref.shape[1] // LANES, group, 0)
    for copy in copies:
        copy.wait()


def own_gather(table, ninth, conn, oper, listed, counts, send):
    elems = conn.shape[1]
    copied = [jax.ShapeDtypeStruct(x.shape, x.dtype) for x in (oper, listed, counts, send)]
    return pl.pallas_call(
        own_gather_kernel,
        out_shape=(
            jax.ShapeDtypeStruct((10, 8, elems), jnp.float32),
            jax.ShapeDtypeStruct((10, elems), jnp.float32),
            *copied,
        ),
        in_specs=[VMEM] * 3 + [HBM] * 4,
        out_specs=(VMEM,) * 6,
        scratch_shapes=[pltpu.SemaphoreType.DMA((4,))],
        compiler_params=pltpu.CompilerParams(vmem_limit_bytes=LIMIT),
        cost_estimate=pl.CostEstimate(flops=20000000, bytes_accessed=4000000, transcendentals=0),
        name="own_gather",
    )(table, ninth, conn, oper, listed, counts, send)


def block_kernel(
    first_halo, first_ref, last_ref, conn_ref, oper_ref, h0_ref, h1_ref, h2_ref, send_ref,
    blk_ref, prev_ref, next_ref, other_ref, ninth_ref, full_ref,
):
    halos = (h0_ref, h1_ref, h2_ref)
    for side, ref in enumerate(halos):
        ninth_ref[side:side + 1, :] = ref[8:9, :]
    sub = lax.broadcasted_iota(jnp.int32, (8, LANES), 0)
    groups = conn_ref.shape[1] // LANES

    def group(block, slot):
        lanes = pl.ds(pl.multiple_of(block * LANES, LANES), LANES)
        corners, edges = [], []
        for node in range(10):
            index = rows8(conn_ref, node, lanes)
            low, high = index & 127, index >> 7
            first = first_ref[node, :, lanes]
            for side in range(3):
                first = jnp.where(high == first_halo + side, lane_gather(halos[side][0:8, :], low), first)
            (corners if node < 4 else edges).append(first)
            full_ref[slot, node, 0:8, :] = first
            last = jnp.where(high == sub + first_halo, lane_gather(ninth_ref[...], low), 0.0)
            full_ref[slot, node, 8:16, :] = jnp.where(sub == 3, rows8(last_ref, node, lanes), last)
        totals = [[jnp.zeros((8, LANES), jnp.float32) for _ in range(3)] for _ in range(2)]
        for node in range(10):
            for comp in range(3):
                oper = oper_ref[3 * node + comp, :, lanes].astype(jnp.float32)
                for step in range(2):
                    row = 3 + 3 * step + comp
                    value = jnp.broadcast_to(full_ref[slot, node, row:row + 1, :], (8, LANES))
                    if row == 8:
                        for extra in (9, 10, 11):
                            value = value + jnp.broadcast_to(full_ref[slot, node, extra:extra + 1, :], (8, LANES))
                    for part in range(3):
                        totals[step][part] = totals[step][part] + oper[8 * part:8 * part + 8] * value
        for step in range(2):
            for part in range(3):
                row = 24 * step + 8 * part
                blk_ref[row:row + 8, lanes] = totals[step][part]
        points = []
        for quad in range(4):
            total = corners[0] * SHAPE[quad, 0]
            for node in range(1, 10):
                total = total + (corners + edges)[node] * SHAPE[quad, node]
            points.append(total)
        blk_ref[48:56, lanes] = jnp.where(sub < 4, points[0], pltpu.roll(points[1], 4, 0))
        blk_ref[56:64, lanes] = jnp.where(sub < 4, points[2], pltpu.roll(points[3], 4, 0))

    def pair(block, carry):
        for slot in range(UNROLL):
            group(block * UNROLL + slot, slot)
        return carry

    lax.fori_loop(0, groups // UNROLL, pair, 0)
    for side, out_ref in enumerate((prev_ref, next_ref, other_ref)):
        index = jnp.broadcast_to(send_ref[side], (8, LANES))
        low, high = index & 127, index >> 7
        hits = [high == chunk for chunk in range(groups)]
        for row in range(0, 64, 8):
            total = jnp.zeros((8, LANES), jnp.float32)
            for chunk in range(groups):
                piece = blk_ref[row:row + 8, chunk * LANES:(chunk + 1) * LANES]
                total = jnp.where(hits[chunk], lane_gather(piece, low), total)
            out_ref[row:row + 8, :] = total


def make_blocks(first, last, conn, oper, halos, send, first_halo):
    elems = conn.shape[1]
    out = jax.ShapeDtypeStruct((64, LANES), jnp.float32)

    def kernel(*refs):
        block_kernel(first_halo, *refs)

    return pl.pallas_call(
        kernel,
        out_shape=(jax.ShapeDtypeStruct((64, elems), jnp.float32), out, out, out),
        in_specs=[VMEM] * 8,
        out_specs=(VMEM,) * 4,
        scratch_shapes=[
            pltpu.VMEM((8, LANES), jnp.float32),
            pltpu.VMEM((UNROLL, 10, 16, LANES), jnp.float32),
        ],
        compiler_params=pltpu.CompilerParams(vmem_limit_bytes=LIMIT),
        name="make_blocks",
    )(first, last, conn, oper, *halos, send)


def add_points(sub, piece):
    pair = jnp.where(sub >= 6, piece[0], piece[1])
    later = jnp.where(sub >= 4, piece[1], piece[2])
    return piece[0] + pltpu.roll(pair, 2, 0) + pltpu.roll(later, 4, 0) + pltpu.roll(piece[2], 6, 0)


def moment_rows(sub, ref, lanes, out_ref, out_lanes):
    spread = []
    for dim in range(3):
        rows = [rows8(ref, 48 + 4 * quad + dim, lanes) for quad in range(4)]
        spread.append([jnp.where(sub < 6 - 2 * k, rows[k], rows[k + 1]) for k in range(3)])
    for step in range(2):
        piece = [ref[24 * step + 8 * k:24 * step + 8 * k + 8, lanes] for k in range(3)]
        base = 32 * step
        out_ref[base:base + 8, out_lanes] = add_points(sub, piece)
        for dim in range(3):
            scaled = [piece[k] * spread[dim][k] for k in range(3)]
            out_ref[base + 8 * dim + 8:base + 8 * dim + 16, out_lanes] = add_points(sub, scaled)
    pair = [ref[48:56, lanes], ref[56:64, lanes]]
    out_ref[64:72, out_lanes] = pair[0] + pair[1]
    out_ref[72:80, out_lanes] = pair[0] * pair[0] + pair[1] * pair[1]
    for shift in (1, 2):
        total = pair[0] * pltpu.roll(pair[0], 8 - shift, 0) + pair[1] * pltpu.roll(pair[1], 8 - shift, 0)
        out_ref[72 + 8 * shift:80 + 8 * shift, out_lanes] = total


def summed_over(moments, weights, weight_dim):
    total = None
    rest = moments
    for part in range(3):
        piece = rest.astype(jnp.bfloat16)
        if part < 2:
            rest = rest - piece.astype(jnp.float32)
        term = lax.dot_general(
            piece, weights, (((1,), (weight_dim,)), ((), ())), preferred_element_type=jnp.float32
        )
        total = term if total is None else total + term
    return total


def sum_kernel(
    list_ref, count_ref, blk_ref, sum_ref, halo_ref, index_ref, hist_ref, weight_ref, moment_ref
):
    patches, slots = list_ref.shape
    counts = count_ref[...].astype(jnp.float32)
    diagonal = lax.broadcasted_iota(jnp.int32, (patches, patches), 0) == lax.broadcasted_iota(
        jnp.int32, (patches, patches), 1
    )
    spread = jnp.where(diagonal, jnp.broadcast_to(counts, (patches, patches)), 0.0)
    limits = jnp.dot(
        spread.astype(jnp.bfloat16),
        jnp.ones((patches, slots), jnp.bfloat16),
        preferred_element_type=jnp.float32,
    ).astype(jnp.int32)
    slot = lax.broadcasted_iota(jnp.int32, (patches, slots), 1)
    index_ref[...] = jnp.where(slot < limits, list_ref[...], 4095)
    low_ids = lax.broadcasted_iota(jnp.int32, (LANES, slots), 0)
    high_ids = lax.broadcasted_iota(jnp.int32, (16, slots), 0)
    width = WIDTH

    def group(block, carry):
        start = pl.multiple_of(block * width, width)
        listed = index_ref[pl.ds(start, width), :]
        low, high = listed & 127, listed >> 7
        for patch in range(width):
            low_hit = low_ids == jnp.broadcast_to(low[patch:patch + 1], (LANES, slots))
            high_hit = high_ids == jnp.broadcast_to(high[patch:patch + 1], (16, slots))
            hist = lax.dot_general(
                jnp.where(high_hit, 1.0, 0.0).astype(jnp.float8_e4m3fn),
                jnp.where(low_hit, 1.0, 0.0).astype(jnp.float8_e4m3fn),
                (((1,), (1,)), ((), ())),
                preferred_element_type=jnp.float32,
            )
            hist_ref[pl.ds(pl.multiple_of(start * 16, LANES) + 16 * patch, 16), :] = hist
        return carry

    lax.fori_loop(0, patches // width, group, 0)
    elems = blk_ref.shape[1]
    chunks = elems // LANES
    for chunk in range(chunks + 3):
        column = hist_ref[pl.ds(chunk, patches, stride=16), :]
        if chunk < chunks:
            weight_ref[:, chunk * LANES:(chunk + 1) * LANES] = column.astype(jnp.bfloat16)
        else:
            row = (chunk - chunks) * LANES
            halo_ref[row:row + LANES, :] = column.T.astype(jnp.bfloat16)
    sub = lax.broadcasted_iota(jnp.int32, (8, LANES), 0)

    def moments(block, carry):
        lanes = pl.ds(pl.multiple_of(block * LANES, LANES), LANES)
        moment_rows(sub, blk_ref, lanes, moment_ref, lanes)
        return carry

    lax.fori_loop(0, chunks, moments, 0)
    sum_ref[...] = summed_over(moment_ref[...], weight_ref[...], 1)


def own_sums(listed, counts, blk):
    patches, slots = listed.shape
    elems = blk.shape[1]
    return pl.pallas_call(
        sum_kernel,
        out_shape=(
            jax.ShapeDtypeStruct((96, patches), jnp.float32),
            jax.ShapeDtypeStruct((3 * LANES, patches), jnp.bfloat16),
        ),
        in_specs=[VMEM] * 3,
        out_specs=(VMEM,) * 2,
        scratch_shapes=[
            pltpu.VMEM((patches, slots), jnp.int32),
            pltpu.VMEM((patches * 16, LANES), jnp.float32),
            pltpu.VMEM((patches, elems), jnp.bfloat16),
            pltpu.VMEM((96, elems), jnp.float32),
        ],
        compiler_params=pltpu.CompilerParams(vmem_limit_bytes=LIMIT),
        cost_estimate=pl.CostEstimate(flops=40000000, bytes_accessed=8000000, transcendentals=0),
        name="own_sums",
    )(listed, counts, blk)


def fit_kernel(sum_ref, weight_ref, h0_ref, h1_ref, h2_ref, vertex_ref, count_ref, out_ref, moment_ref, total_ref):
    sub = lax.broadcasted_iota(jnp.int32, (8, LANES), 0)
    for side, ref in enumerate((h0_ref, h1_ref, h2_ref)):
        moment_rows(sub, ref, slice(0, LANES), moment_ref, slice(side * LANES, (side + 1) * LANES))
    patches = weight_ref.shape[1]
    total_ref[...] = sum_ref[...] + summed_over(moment_ref[...], weight_ref[...], 0)

    def row(ref, start):
        return jnp.broadcast_to(ref[start:start + 1, 0:patches], (8, patches))

    def both(start):
        return row(total_ref, start) + row(total_ref, start + 4)

    points = 4.0 * row(count_ref, 0).astype(jnp.float32)
    vertex = [row(vertex_ref, dim) for dim in range(3)]
    sum_x = [both(64 + dim) for dim in range(3)]
    sum_xx = {
        (0, 0): both(72), (1, 1): both(73), (2, 2): both(74),
        (0, 1): both(80), (1, 2): both(81), (0, 2): both(88),
    }
    gram = {(0, 0): points + RIDGE}
    for a in range(3):
        gram[0, a + 1] = sum_x[a] - points * vertex[a]
        for b in range(a, 3):
            value = sum_xx[a, b] - vertex[a] * sum_x[b] - sum_x[a] * vertex[b] + points * vertex[a] * vertex[b]
            gram[a + 1, b + 1] = value + RIDGE if a == b else value
    rhs = []
    for step in range(2):
        base = total_ref[32 * step:32 * step + 8, :]
        rest = [total_ref[32 * step + 8 * dim + 8:32 * step + 8 * dim + 16, :] for dim in range(3)]
        rhs.append([base] + [rest[dim] - vertex[dim] * base for dim in range(3)])
    for pivot in (3, 2, 1):
        inverse = 1.0 / gram[pivot, pivot]
        for other in range(pivot):
            factor = gram[other, pivot] * inverse
            for column in range(other, pivot):
                gram[other, column] = gram[other, column] - factor * gram[column, pivot]
            for step in range(2):
                rhs[step][other] = rhs[step][other] - factor * rhs[step][pivot]
    inverse = 1.0 / gram[0, 0]
    for step in range(2):
        out_ref[6 * step:6 * step + 6, :] = (rhs[step][0] * inverse)[0:6]


def fit(sums, weights, halos, coords, counts):
    patches = weights.shape[1]
    return pl.pallas_call(
        fit_kernel,
        out_shape=jax.ShapeDtypeStruct((12, patches), jnp.float32),
        in_specs=[VMEM] * 7,
        out_specs=VMEM,
        scratch_shapes=[
            pltpu.VMEM((96, 3 * LANES), jnp.float32),
            pltpu.VMEM((96, patches), jnp.float32),
        ],
        compiler_params=pltpu.CompilerParams(vmem_limit_bytes=LIMIT),
        name="fit",
    )(sums, weights, *halos, coords, counts)


def exchange(to_prev, to_next, to_other):
    count = lax.axis_size("dom")
    up = [(i, (i + 1) % count) for i in range(count)]
    down = [(j, i) for i, j in up]
    swap = [(0, 1), (1, 0)]
    from_prev = lax.ppermute(to_next, "dom", up)
    from_next = lax.ppermute(to_prev, "dom", down)
    from_other = lax.ppermute(to_other, "slab", swap)
    return from_prev, from_next, from_other


def local(coords, disp, oper, conn, node_send, element_send, patch_elements, patch_count):
    node_send = node_send.transpose(1, 0, 2)
    element_send = element_send.transpose(1, 0, 2)
    oper = oper.transpose(1, 0, 2)
    listed = patch_elements.T
    far = [pltpu.with_memory_space_constraint(x, pltpu.HBM) for x in (
        coords, disp, node_send, conn, oper, listed, patch_count, element_send
    )]
    *picked, table, ninth, coords_near, conn_near = node_pick(*far[0:4])
    halos = exchange(*picked)
    first, last, oper, listed, counts, send = own_gather(
        table, ninth, conn_near, *far[4:8]
    )
    blk, *picked = make_blocks(first, last, conn_near, oper, halos, send, coords.shape[1] // LANES)
    halos = exchange(*picked)
    sums, weights = own_sums(listed, counts, blk)
    return fit(sums, weights, halos, coords_near, counts)


def solution(mesh):
    both = ("dom", "slab")
    in_specs = (
        P(None, both),
        P(None, both),
        P(None, None, both),
        P(None, both),
        P(both, None, None),
        P(both, None, None),
        P(None, both),
        P(both, None),
    )
    return jax.shard_map(local, mesh=mesh, in_specs=in_specs, out_specs=P(None, both), check_vma=False)
```

time: 40.2 us -> 28.5 us (0.71)
  local copies, waits for them, and re-layouts: 5.94 us -> 0 us
  Pallas kernels: 14.1 us -> 8.59 us
    unnamed x20 -> x0, local copies, waits for them, and re-layouts: 5.94 us -> none
    pallas_call x4 -> x3, Pallas kernels: 10.2 us -> 6.18 us  [the longest x1 3.24 us: own_sums(): pl.pallas_call(sum_kernel, out_shape=(jax.ShapeDtypeStruct((96, patches),...]
    pallas_call x1, Pallas kernels: 2.9 us -> 1.51 us  [make_blocks(): pl.pallas_call(kernel, out_shape=(jax.ShapeDtypeStruct((64, elems), jnp.f...]
  transfers between devices with their start and end apart: 6 -> 6, of which waited for: 0 -> 0; matrix products, arithmetic and copies ran while one was open for 0% -> 0% of each run, Pallas kernels for 25% -> 18%
where the time goes in v1:
time: 28.5 us; the launch traced here: 28.4 us
  starting transfers between devices  19.7 us (69%)
  Pallas kernels  8.59 us (30%)
    ppermute x2, starting transfers between devices, exchange(): from_next = lax.ppermute(to_prev, 'dom', down)  16 us
    pallas_call x1, Pallas kernels, own_sums(): pl.pallas_call(sum_kernel, out_shape=(jax.ShapeDtypeStruct((96, patches),...  3.24 us
    ppermute x2, starting transfers between devices, exchange(): from_prev = lax.ppermute(to_next, 'dom', up)  2.2 us
    pallas_call x1, Pallas kernels, own_gather(): pl.pallas_call(own_gather_kernel, out_shape=(jax.ShapeDtypeStruct((10, 8,...  1.97 us
    ppermute x2, starting transfers between devices, exchange(): from_other = lax.ppermute(to_other, 'slab', swap)  1.52 us
    pallas_call x1, Pallas kernels, make_blocks(): pl.pallas_call(kernel, out_shape=(jax.ShapeDtypeStruct((64, elems), jnp.f...  1.51 us
    pallas_call x1, Pallas kernels, node_pick(): pl.pallas_call(node_pick_kernel, out_shape=(out, out, out, jax.ShapeDtype...  0.97 us
    pallas_call x1, Pallas kernels, fit(): pl.pallas_call(fit_kernel, out_shape=jax.ShapeDtypeStruct((12, patches),...  0.9 us
  transfers between devices with their start and end apart: 6, of which 0 were waited for; matrix products, arithmetic and copies ran while one was open for 0% of the time, Pallas kernels for 18%

profile of v1, /device:TPU:1, one launch (start us, length us, event | category | flops | bytes accessed | tf_op | source)
XLA Modules:
  0.0 28.4 jit_solution(14815134484384955709)
XLA Ops:
  0.0 1.0 %node_pick.1 = (f32[9,128]{1,0:T(8,128)S(1)}, f32[9,128]{1,0:T(8,128)S(1)}, f32[9,128]{1,0:T(8,128)S(1)}, f32[11,8,128]{2,1,0:T(8,128)S(1)}, f32[16,128]{1,0:T(8...) custom-call(f32[3,1408]{1,0:T(4,128)} %coords_hbm.1, f32[6,1408]{1,0:T(8,128)} %disp_hbm.1, ...), custom_call_target="tpu_custom_call" | custom-call | tf_op jit(solution)/shard_map/node_pick/pallas_call | solution.py:90
  1.0 2.1 %collective-permute-start = (f32[9,128]{1,0:T(8,128)S(1)}, f32[9,128]{1,0:T(8,128)S(1)}, u32[]{:S(2)}, u32[]{:S(2)}) collective-permute-start(f32[9,128]{1,0:T(8,128)S(1)} %get-tuple-element.32), channel_id=1, source_target_pairs={{0,2},{2,4},{4,6},{6,8},{8,10},{10,12},{12,14},{14,16},{16,18},{18... | collective-permute-start | bytes 13832 | tf_op jit(solution)/shard_map/ppermute | solution.py:429
  3.1 9.1 %collective-permute-start.1 = (f32[9,128]{1,0:T(8,128)S(1)}, f32[9,128]{1,0:T(8,128)S(1)}, u32[]{:S(2)}, u32[]{:S(2)}) collective-permute-start(f32[9,128]{1,0:T(8,128)S(1)} %get-tuple-element.33), channel_id=1, source_target_pairs={{2,0},{4,2},{6,4},{8,6},{10,8},{12,10},{14,12},{16,14},{18,16},{20... | collective-permute-start | bytes 13832 | tf_op jit(solution)/shard_map/ppermute | solution.py:430
  12.2 1.0 %collective-permute-start.2 = (f32[9,128]{1,0:T(8,128)S(1)}, f32[9,128]{1,0:T(8,128)S(1)}, u32[]{:S(2)}, u32[]{:S(2)}) collective-permute-start(f32[9,128]{1,0:T(8,128)S(1)} %get-tuple-element.34), channel_id=1, source_target_pairs={{0,1},{1,0},{2,3},{3,2},{4,5},{5,4},{6,7},{7,6},{8,9},{9,8},{10,11... | collective-permute-start | bytes 13832 | tf_op jit(solution)/shard_map/ppermute | solution.py:431
  13.2 2.0 %own_gather.1 = (f32[10,8,1024]{2,1,0:T(8,128)S(1)}, f32[10,1024]{1,0:T(8,128)S(1)}, bf16[30,24,1024]{2,1,0:T(8,128)(2,1)S(1)}, s32[192,128]{1,0:T(8,128)S(1)}, ...) custom-call(f32[11,8,128]{2,1,0:T(8,128)S(1)} %get-tuple-element.24.table_ref, f32[16,128]{1,0:T(8,128)S(1)} %get-tuple-element.25.ninth_ref, ...), custom_call_target="tpu_custom_call" | custom-call | flops 20000000 | bytes 4000000 | tf_op jit(solution)/shard_map/own_gather/pallas_call | solution.py:141
  15.1 0.0 collective-permute-done.refs_4_
  15.1 0.0 collective-permute-done.1.refs_5_
  15.1 0.0 collective-permute-done.2.refs_6_
  15.2 1.5 %make_blocks.1 = (f32[64,1024]{1,0:T(8,128)S(1)}, f32[64,128]{1,0:T(8,128)S(1)}, f32[64,128]{1,0:T(8,128)S(1)}, f32[64,128]{1,0:T(8,128)S(1)}) custom-call(f32[10,8,1024]{2,1,0:T(8,128)S(1)} %get-tuple-element.29.refs_0_, f32[10,1024]{1,0:T(8,128)S(1)} %get-tuple-element.30.refs_1_, s32[10,1024]{1,0:T(8,128)S(1)} %get-tuple-element.26.conn_ref.refs_2_, ...), custom_call_target="tpu_custom_call" | custom-call | tf_op jit(solution)/shard_map/make_blocks/pallas_call | solution.py:230
  16.7 0.1 collective-permute-start.3
  16.8 6.9 %collective-permute-start.4 = (f32[64,128]{1,0:T(8,128)S(1)}, f32[64,128]{1,0:T(8,128)S(1)}, u32[]{:S(2)}, u32[]{:S(2)}) collective-permute-start(f32[64,128]{1,0:T(8,128)S(1)} %get-tuple-element.40), channel_id=1, source_target_pairs={{2,0},{4,2},{6,4},{8,6},{10,8},{12,10},{14,12},{16,14},{18,16},{20... | collective-permute-start | bytes 98312 | tf_op jit(solution)/shard_map/ppermute | solution.py:430
  23.6 0.6 %collective-permute-start.5 = (f32[64,128]{1,0:T(8,128)S(1)}, f32[64,128]{1,0:T(8,128)S(1)}, u32[]{:S(2)}, u32[]{:S(2)}) collective-permute-start(f32[64,128]{1,0:T(8,128)S(1)} %get-tuple-element.41), channel_id=1, source_target_pairs={{0,1},{1,0},{2,3},{3,2},{4,5},{5,4},{6,7},{7,6},{8,9},{9,8},{10,11... | collective-permute-start | bytes 98312 | tf_op jit(solution)/shard_map/ppermute | solution.py:431
  24.2 3.2 %own_sums.1 = (f32[96,192]{1,0:T(8,128)S(1)}, bf16[384,192]{1,0:T(8,128)(2,1)S(1)}) custom-call(s32[192,128]{1,0:T(8,128)S(1)} %get-tuple-element.27.list_ref, s32[1,192]{1,0:T(1,128)S(1)} %get-tuple-element.28.count_ref, f32[64,1024]{1,0:T(8,128)S(1)} %get-tuple-element.36.blk_ref), custom_call_target="tpu_custom_call" | custom-call | flops 40000000 | bytes 8000000 | tf_op jit(solution)/shard_map/own_sums/pallas_call | solution.py:344
  27.5 0.0 collective-permute-done.3.h0_ref
  27.5 0.0 collective-permute-done.4.h1_ref
  27.5 0.0 collective-permute-done.5.h2_ref
  27.5 0.9 %fit.1 = f32[12,192]{1,0:T(8,128)} custom-call(f32[96,192]{1,0:T(8,128)S(1)} %get-tuple-element.37.sum_ref, bf16[384,192]{1,0:T(8,128)(2,1)S(1)} %get-tuple-element.38.weight_ref, f32[64,128]{1,0:T(8,128)S(1)} %collective-permute-done.3.h0_ref, f32[64,128]{1,0:T(8,128)S(1)} %collective-permute-done.4.h1_ref, f32[64,128]{1,0:T(8,128)S(1)} %collective-permute-done.5.h2_ref, ...), custom_call_target="tpu_custom_call" | custom-call | tf_op jit(solution)/shard_map/fit/pallas_call | solution.py:410
Async XLA Ops:
  1.0 14.2 %collective-permute-start = (f32[9,128]{1,0:T(8,128)S(1)}, f32[9,128]{1,0:T(8,128)S(1)}, u32[]{:S(2)}, u32[]{:S(2)}) collective-permute-start(f32[9,128]{1,0:T(8,128)S(1)} %get-tuple-element.32), channel_id=1, source_target_pairs={{0,2},{2,4},{4,6},{6,8},{8,10},{10,12},{12,14},{14,16},{16,18},{18... | collective-permute-start | bytes 13832 | tf_op jit(solution)/shard_map/ppermute | solution.py:429
  3.1 12.0 %collective-permute-start.1 = (f32[9,128]{1,0:T(8,128)S(1)}, f32[9,128]{1,0:T(8,128)S(1)}, u32[]{:S(2)}, u32[]{:S(2)}) collective-permute-start(f32[9,128]{1,0:T(8,128)S(1)} %get-tuple-element.33), channel_id=1, source_target_pairs={{2,0},{4,2},{6,4},{8,6},{10,8},{12,10},{14,12},{16,14},{18,16},{20... | collective-permute-start | bytes 13832 | tf_op jit(solution)/shard_map/ppermute | solution.py:430
  12.2 3.0 %collective-permute-start.2 = (f32[9,128]{1,0:T(8,128)S(1)}, f32[9,128]{1,0:T(8,128)S(1)}, u32[]{:S(2)}, u32[]{:S(2)}) collective-permute-start(f32[9,128]{1,0:T(8,128)S(1)} %get-tuple-element.34), channel_id=1, source_target_pairs={{0,1},{1,0},{2,3},{3,2},{4,5},{5,4},{6,7},{7,6},{8,9},{9,8},{10,11... | collective-permute-start | bytes 13832 | tf_op jit(solution)/shard_map/ppermute | solution.py:431
  16.7 10.8 %collective-permute-start.3 = (f32[64,128]{1,0:T(8,128)S(1)}, f32[64,128]{1,0:T(8,128)S(1)}, u32[]{:S(2)}, u32[]{:S(2)}) collective-permute-start(f32[64,128]{1,0:T(8,128)S(1)} %get-tuple-element.39), channel_id=1, source_target_pairs={{0,2},{2,4},{4,6},{6,8},{8,10},{10,12},{12,14},{14,16},{16,18},{18... | collective-permute-start | bytes 98312 | tf_op jit(solution)/shard_map/ppermute | solution.py:429
  16.8 10.7 %collective-permute-start.4 = (f32[64,128]{1,0:T(8,128)S(1)}, f32[64,128]{1,0:T(8,128)S(1)}, u32[]{:S(2)}, u32[]{:S(2)}) collective-permute-start(f32[64,128]{1,0:T(8,128)S(1)} %get-tuple-element.40), channel_id=1, source_target_pairs={{2,0},{4,2},{6,4},{8,6},{10,8},{12,10},{14,12},{16,14},{18,16},{20... | collective-permute-start | bytes 98312 | tf_op jit(solution)/shard_map/ppermute | solution.py:430
  23.6 3.8 %collective-permute-start.5 = (f32[64,128]{1,0:T(8,128)S(1)}, f32[64,128]{1,0:T(8,128)S(1)}, u32[]{:S(2)}, u32[]{:S(2)}) collective-permute-start(f32[64,128]{1,0:T(8,128)S(1)} %get-tuple-element.41), channel_id=1, source_target_pairs={{0,1},{1,0},{2,3},{3,2},{4,5},{5,4},{6,7},{7,6},{8,9},{9,8},{10,11... | collective-permute-start | bytes 98312 | tf_op jit(solution)/shard_map/ppermute | solution.py:431

commit v2 on v1

--- a/solution.py
+++ b/solution.py
@@ -12,6 +12,7 @@
 HBM = pl.BlockSpec(memory_space=pltpu.HBM)
 UNROLL = 2
 WIDTH = 64
+EDGE = 4
 LIMIT = 24 * 1024 * 1024
 
 
@@ -108,12 +109,13 @@
     )(coords, disp, send, conn)
 
 
-def own_gather_kernel(
-    table_ref, ninth_ref, conn_ref, oper_hbm, list_hbm, count_hbm, send_hbm,
-    first_ref, last_ref, oper_ref, list_ref, count_ref, send_ref, sems,
-):
-    pairs = ((oper_hbm, oper_ref), (list_hbm, list_ref), (count_hbm, count_ref), (send_hbm, send_ref))
-    copies = start_all(pairs, sems)
+def at_edge():
+    return lax.rem(lax.axis_index("dom"), EDGE) == 0
+
+
+def gather_work(table_ref, ninth_ref, conn_ref, far, near, sems):
+    first_ref, last_ref = near[0:2]
+    copies = start_all(tuple(zip(far, near[2:6])), sems)
     sub = lax.broadcasted_iota(jnp.int32, (8, LANES), 0)
     chunks = table_ref.shape[0]
 
@@ -135,23 +137,47 @@
         copy.wait()
 
 
-def own_gather(table, ninth, conn, oper, listed, counts, send):
+def early_gather_kernel(*refs):
+    held, outs, sems = refs[7:9], refs[15:17], refs[17]
+    for source, target in zip(held, outs):
+        target[...] = source[...]
+
+    @pl.when(at_edge())
+    def _():
+        gather_work(*refs[0:3], refs[3:7], refs[9:15], sems)
+
+
+def late_gather_kernel(*refs):
+    sems = refs[19]
+    done, near = refs[7:13], refs[13:19]
+
+    @pl.when(at_edge())
+    def _():
+        for source, target in zip(done, near):
+            target[...] = source[...]
+
+    @pl.when(jnp.logical_not(at_edge()))
+    def _():
+        gather_work(*refs[0:3], refs[3:7], near, sems)
+
+
+def own_gather(table, ninth, conn, far, held=None, done=None):
     elems = conn.shape[1]
-    copied = [jax.ShapeDtypeStruct(x.shape, x.dtype) for x in (oper, listed, counts, send)]
+    outs = [jax.ShapeDtypeStruct((10, 8, elems), jnp.float32), jax.ShapeDtypeStruct((10, elems), jnp.float32)]
+    outs = outs + [jax.ShapeDtypeStruct(x.shape, x.dtype) for x in far]
+    extra = list(done) if held is None else list(held)
+    if held is not None:
+        outs = outs + [jax.ShapeDtypeStruct(x.shape, x.dtype) for x in held]
     return pl.pallas_call(
-        own_gather_kernel,
-        out_shape=(
-            jax.ShapeDtypeStruct((10, 8, elems), jnp.float32),
-            jax.ShapeDtypeStruct((10, elems), jnp.float32),
-            *copied,
-        ),
-        in_specs=[VMEM] * 3 + [HBM] * 4,
-        out_specs=(VMEM,) * 6,
+        late_gather_kernel if held is None else early_gather_kernel,
+        out_shape=tuple(outs),
+        in_specs=[VMEM] * 3 + [HBM] * 4 + [VMEM] * len(extra),
+        out_specs=(VMEM,) * len(outs),
         scratch_shapes=[pltpu.SemaphoreType.DMA((4,))],
         compiler_params=pltpu.CompilerParams(vmem_limit_bytes=LIMIT),
         cost_estimate=pl.CostEstimate(flops=20000000, bytes_accessed=4000000, transcendentals=0),
-        name="own_gather",
-    )(table, ninth, conn, oper, listed, counts, send)
+        name="late_gather" if held is None else "early_gather",
+    )(table, ninth, conn, *far, *extra)
 
 
 def block_kernel(
@@ -281,7 +307,7 @@
     return total
 
 
-def sum_kernel(
+def sum_work(
     list_ref, count_ref, blk_ref, sum_ref, halo_ref, index_ref, hist_ref, weight_ref, moment_ref
 ):
     patches, slots = list_ref.shape
@@ -338,17 +364,43 @@
     sum_ref[...] = summed_over(moment_ref[...], weight_ref[...], 1)
 
 
-def own_sums(listed, counts, blk):
+def early_sum_kernel(
+    list_ref, count_ref, blk_ref, prev_ref, other_ref, sum_ref, halo_ref, prev_out, other_out, *scratch
+):
+    prev_out[...] = prev_ref[...]
+    other_out[...] = other_ref[...]
+
+    @pl.when(at_edge())
+    def _():
+        sum_work(list_ref, count_ref, blk_ref, sum_ref, halo_ref, *scratch)
+
+
+def late_sum_kernel(list_ref, count_ref, blk_ref, sum_in, halo_in, sum_ref, halo_ref, *scratch):
+    @pl.when(at_edge())
+    def _():
+        sum_ref[...] = sum_in[...]
+        halo_ref[...] = halo_in[...]
+
+    @pl.when(jnp.logical_not(at_edge()))
+    def _():
+        sum_work(list_ref, count_ref, blk_ref, sum_ref, halo_ref, *scratch)
+
+
+def own_sums(listed, counts, blk, held=None, done=None):
     patches, slots = listed.shape
     elems = blk.shape[1]
+    outs = [
+        jax.ShapeDtypeStruct((96, patches), jnp.float32),
+        jax.ShapeDtypeStruct((3 * LANES, patches), jnp.bfloat16),
+    ]
+    extra = list(done) if held is None else list(held)
+    if held is not None:
+        outs = outs + [jax.ShapeDtypeStruct(x.shape, x.dtype) for x in held]
     return pl.pallas_call(
-        sum_kernel,
-        out_shape=(
-            jax.ShapeDtypeStruct((96, patches), jnp.float32),
-            jax.ShapeDtypeStruct((3 * LANES, patches), jnp.bfloat16),
-        ),
-        in_specs=[VMEM] * 3,
-        out_specs=(VMEM,) * 2,
+        late_sum_kernel if held is None else early_sum_kernel,
+        out_shape=tuple(outs),
+        in_specs=[VMEM] * (3 + len(extra)),
+        out_specs=(VMEM,) * len(outs),
         scratch_shapes=[
             pltpu.VMEM((patches, slots), jnp.int32),
             pltpu.VMEM((patches * 16, LANES), jnp.float32),
@@ -357,8 +409,8 @@
         ],
         compiler_params=pltpu.CompilerParams(vmem_limit_bytes=LIMIT),
         cost_estimate=pl.CostEstimate(flops=40000000, bytes_accessed=8000000, transcendentals=0),
-        name="own_sums",
-    )(listed, counts, blk)
+        name="late_sums" if held is None else "early_sums",
+    )(listed, counts, blk, *extra)
 
 
 def fit_kernel(sum_ref, weight_ref, h0_ref, h1_ref, h2_ref, vertex_ref, count_ref, out_ref, moment_ref, total_ref):
@@ -421,15 +473,16 @@
     )(sums, weights, *halos, coords, counts)
 
 
-def exchange(to_prev, to_next, to_other):
+def exchange(to_prev, to_next, to_other, early):
     count = lax.axis_size("dom")
     up = [(i, (i + 1) % count) for i in range(count)]
     down = [(j, i) for i, j in up]
     swap = [(0, 1), (1, 0)]
     from_prev = lax.ppermute(to_next, "dom", up)
+    *done, to_prev, to_other = early((to_prev, to_other))
     from_next = lax.ppermute(to_prev, "dom", down)
     from_other = lax.ppermute(to_other, "slab", swap)
-    return from_prev, from_next, from_other
+    return (from_prev, from_next, from_other), done
 
 
 def local(coords, disp, oper, conn, node_send, element_send, patch_elements, patch_count):
@@ -441,13 +494,13 @@
         coords, disp, node_send, conn, oper, listed, patch_count, element_send
     )]
     *picked, table, ninth, coords_near, conn_near = node_pick(*far[0:4])
-    halos = exchange(*picked)
-    first, last, oper, listed, counts, send = own_gather(
-        table, ninth, conn_near, *far[4:8]
-    )
+    own = (table, ninth, conn_near, far[4:8])
+    halos, done = exchange(*picked, lambda held: own_gather(*own, held=held))
+    first, last, oper, listed, counts, send = own_gather(*own, done=done)
     blk, *picked = make_blocks(first, last, conn_near, oper, halos, send, coords.shape[1] // LANES)
-    halos = exchange(*picked)
-    sums, weights = own_sums(listed, counts, blk)
+    own = (listed, counts, blk)
+    halos, done = exchange(*picked, lambda held: own_sums(*own, held=held))
+    sums, weights = own_sums(*own, done=done)
     return fit(sums, weights, halos, coords_near, counts)
 
 

time: 28.5 us -> 25.9 us (0.909)
  starting transfers between devices: 19.7 us -> 15.4 us
  waiting for transfers between devices: 0.02 us -> 1.45 us
    ppermute x2, starting transfers between devices: 16 us -> 10.8 us  [exchange(): from_next = lax.ppermute(to_prev, 'dom', down)]
    ppermute x2, waiting for transfers between devices: 0.01 us -> 1.44 us  [exchange(): from_other = lax.ppermute(to_other, 'slab', swap)]
    ppermute x2, starting transfers between devices: 1.52 us -> 2.43 us  [exchange(): from_other = lax.ppermute(to_other, 'slab', swap)]
    pallas_call x2 -> x4, Pallas kernels: 5.21 us -> 5.4 us  [the longest x2 3.28 us: own_sums(): pl.pallas_call(late_sum_kernel if held is None else early_sum_kernel, out...]
  transfers between devices with their start and end apart: 6 -> 6, of which waited for: 0 -> 2; matrix products, arithmetic and copies ran while one was open for 0% -> 0% of each run, Pallas kernels for 18% -> 21%
where the time goes in v2:
time: 25.9 us; the launch traced here: 25.8 us
  starting transfers between devices  15.4 us (59%)
  Pallas kernels  8.78 us (34%)
  waiting for transfers between devices  1.45 us (6%)
    ppermute x2, starting transfers between devices, exchange(): from_next = lax.ppermute(to_prev, 'dom', down)  10.8 us
    pallas_call x2, Pallas kernels, own_sums(): pl.pallas_call(late_sum_kernel if held is None else early_sum_kernel, out...  3.28 us
    ppermute x2, starting transfers between devices, exchange(): from_other = lax.ppermute(to_other, 'slab', swap)  2.43 us
    ppermute x2, starting transfers between devices, exchange(): from_prev = lax.ppermute(to_next, 'dom', up)  2.2 us
    pallas_call x2, Pallas kernels, own_gather(): pl.pallas_call(late_gather_kernel if held is None else early_gather_kerne...  2.12 us
    pallas_call x1, Pallas kernels, make_blocks(): pl.pallas_call(kernel, out_shape=(jax.ShapeDtypeStruct((64, elems), jnp.f...  1.51 us
    ppermute x2, waiting for transfers between devices, exchange(): from_other = lax.ppermute(to_other, 'slab', swap)  1.44 us
    pallas_call x1, Pallas kernels, node_pick(): pl.pallas_call(node_pick_kernel, out_shape=(out, out, out, jax.ShapeDtype...  0.97 us
  transfers between devices with their start and end apart: 6, of which 2 were waited for; matrix products, arithmetic and copies ran while one was open for 0% of the time, Pallas kernels for 21%

profile of v2, /device:TPU:1, one launch (start us, length us, event | category | flops | bytes accessed | tf_op | source)
XLA Modules:
  0.0 25.8 jit_solution(11245488876082151791)
XLA Ops:
  0.0 1.0 %node_pick.1 = (f32[9,128]{1,0:T(8,128)S(1)}, f32[9,128]{1,0:T(8,128)S(1)}, f32[9,128]{1,0:T(8,128)S(1)}, f32[11,8,128]{2,1,0:T(8,128)S(1)}, f32[16,128]{1,0:T(8...) custom-call(f32[3,1408]{1,0:T(4,128)} %coords_hbm.1, f32[6,1408]{1,0:T(8,128)} %disp_hbm.1, ...), custom_call_target="tpu_custom_call" | custom-call | tf_op jit(solution)/shard_map/node_pick/pallas_call | solution.py:91
  1.0 2.1 %collective-permute-start = (f32[9,128]{1,0:T(8,128)S(1)}, f32[9,128]{1,0:T(8,128)S(1)}, u32[]{:S(2)}, u32[]{:S(2)}) collective-permute-start(f32[9,128]{1,0:T(8,128)S(1)} %get-tuple-element.52), channel_id=1, source_target_pairs={{0,2},{2,4},{4,6},{6,8},{8,10},{10,12},{12,14},{14,16},{16,18},{18... | collective-permute-start | bytes 13832 | tf_op jit(solution)/shard_map/ppermute | solution.py:481
  3.1 2.0 %early_gather.1 = (f32[10,8,1024]{2,1,0:T(8,128)S(1)}, f32[10,1024]{1,0:T(8,128)S(1)}, bf16[30,24,1024]{2,1,0:T(8,128)(2,1)S(1)}, s32[192,128]{1,0:T(8,128)S(1)}...) custom-call(f32[11,8,128]{2,1,0:T(8,128)S(1)} %get-tuple-element.36.refs_0_, ...), custom_call_target="tpu_custom_call" | custom-call | flops 20000000 | bytes 4000000 | tf_op jit(solution)/shard_map/early_gather/pallas_call | solution.py:171
  5.1 7.2 %collective-permute-start.1 = (f32[9,128]{1,0:T(8,128)S(1)}, f32[9,128]{1,0:T(8,128)S(1)}, u32[]{:S(2)}, u32[]{:S(2)}) collective-permute-start(f32[9,128]{1,0:T(8,128)S(1)} %get-tuple-element.53), channel_id=1, source_target_pairs={{2,0},{4,2},{6,4},{8,6},{10,8},{12,10},{14,12},{16,14},{18,16},{20... | collective-permute-start | bytes 13832 | tf_op jit(solution)/shard_map/ppermute | solution.py:483
  12.3 1.0 %collective-permute-start.2 = (f32[9,128]{1,0:T(8,128)S(1)}, f32[9,128]{1,0:T(8,128)S(1)}, u32[]{:S(2)}, u32[]{:S(2)}) collective-permute-start(f32[9,128]{1,0:T(8,128)S(1)} %get-tuple-element.54), channel_id=1, source_target_pairs={{0,1},{1,0},{2,3},{3,2},{4,5},{5,4},{6,7},{7,6},{8,9},{9,8},{10,11... | collective-permute-start | bytes 13832 | tf_op jit(solution)/shard_map/ppermute | solution.py:484
  13.2 0.2 late_gather.1
  13.4 0.0 collective-permute-done.refs_4_
  13.4 0.0 collective-permute-done.1.refs_5_
  13.4 0.6 %collective-permute-done.2.refs_6_ = f32[9,128]{1,0:T(8,128)S(1)} collective-permute-done((f32[9,128]{1,0:T(8,128)S(1)}, f32[9,128]{1,0:T(8,128)S(1)}, u32[]{:S(2)}, u32[]{:S(2)}) %collective-permute-start.2) | collective-permute-done | bytes 4640 | tf_op jit(solution)/shard_map/ppermute | solution.py:484
  14.0 1.5 %make_blocks.1 = (f32[64,1024]{1,0:T(8,128)S(1)}, f32[64,128]{1,0:T(8,128)S(1)}, f32[64,128]{1,0:T(8,128)S(1)}, f32[64,128]{1,0:T(8,128)S(1)}) custom-call(f32[10,8,1024]{2,1,0:T(8,128)S(1)} %get-tuple-element.49.refs_0_, f32[10,1024]{1,0:T(8,128)S(1)} %get-tuple-element.50.refs_1_, s32[10,1024]{1,0:T(8,128)S(1)} %get-tuple-element.38.refs_2_, ...), custom_call_target="tpu_custom_call" | custom-call | tf_op jit(solution)/shard_map/make_blocks/pallas_call | solution.py:256
  15.6 0.1 collective-permute-start.3
  15.7 3.3 %early_sums.1 = (f32[96,192]{1,0:T(8,128)S(1)}, bf16[384,192]{1,0:T(8,128)(2,1)S(1)}, f32[64,128]{1,0:T(8,128)S(1)}, f32[64,128]{1,0:T(8,128)S(1)}) custom-call(s32[192,128]{1,0:T(8,128)S(1)} %get-tuple-element.47.list_ref, s32[1,192]{1,0:T(1,128)S(1)} %get-tuple-element.48.count_ref, f32[64,1024]{1,0:T(8,128)S(1)} %get-tuple-element.56.blk_ref, ...), custom_call_target="tpu_custom_call" | custom-call | flops 40000000 | bytes 8000000 | tf_op jit(solution)/shard_map/early_sums/pallas_call | solution.py:399
  18.9 3.6 %collective-permute-start.4 = (f32[64,128]{1,0:T(8,128)S(1)}, f32[64,128]{1,0:T(8,128)S(1)}, u32[]{:S(2)}, u32[]{:S(2)}) collective-permute-start(f32[64,128]{1,0:T(8,128)S(1)} %get-tuple-element.64), channel_id=1, source_target_pairs={{2,0},{4,2},{6,4},{8,6},{10,8},{12,10},{14,12},{16,14},{18,16},{20... | collective-permute-start | bytes 98312 | tf_op jit(solution)/shard_map/ppermute | solution.py:483
  22.5 1.5 %collective-permute-start.5 = (f32[64,128]{1,0:T(8,128)S(1)}, f32[64,128]{1,0:T(8,128)S(1)}, u32[]{:S(2)}, u32[]{:S(2)}) collective-permute-start(f32[64,128]{1,0:T(8,128)S(1)} %get-tuple-element.65), channel_id=1, source_target_pairs={{0,1},{1,0},{2,3},{3,2},{4,5},{5,4},{6,7},{7,6},{8,9},{9,8},{10,11... | collective-permute-start | bytes 98312 | tf_op jit(solution)/shard_map/ppermute | solution.py:484
  24.0 0.0 collective-permute-done.3.h0_ref
  24.1 0.0 collective-permute-done.4.h1_ref
  24.1 0.8 %collective-permute-done.5.h2_ref = f32[64,128]{1,0:T(8,128)S(1)} collective-permute-done((f32[64,128]{1,0:T(8,128)S(1)}, f32[64,128]{1,0:T(8,128)S(1)}, u32[]{:S(2)}, u32[]{:S(2)}) %collective-permute-start.5) | collective-permute-done | bytes 32800 | tf_op jit(solution)/shard_map/ppermute | solution.py:484
  24.9 0.9 %fit.1 = f32[12,192]{1,0:T(8,128)} custom-call(f32[96,192]{1,0:T(8,128)S(1)} %get-tuple-element.61.sum_ref, bf16[384,192]{1,0:T(8,128)(2,1)S(1)} %get-tuple-element.62.weight_ref, f32[64,128]{1,0:T(8,128)S(1)} %collective-permute-done.3.h0_ref, f32[64,128]{1,0:T(8,128)S(1)} %collective-permute-done.4.h1_ref, f32[64,128]{1,0:T(8,128)S(1)} %collective-permute-done.5.h2_ref, ...), custom_call_target="tpu_custom_call" | custom-call | tf_op jit(solution)/shard_map/fit/pallas_call | solution.py:462
  (1 shorter events, 0.0 us)
Async XLA Ops:
  1.0 12.4 %collective-permute-start = (f32[9,128]{1,0:T(8,128)S(1)}, f32[9,128]{1,0:T(8,128)S(1)}, u32[]{:S(2)}, u32[]{:S(2)}) collective-permute-start(f32[9,128]{1,0:T(8,128)S(1)} %get-tuple-element.52), channel_id=1, source_target_pairs={{0,2},{2,4},{4,6},{6,8},{8,10},{10,12},{12,14},{14,16},{16,18},{18... | collective-permute-start | bytes 13832 | tf_op jit(solution)/shard_map/ppermute | solution.py:481
  5.1 8.3 %collective-permute-start.1 = (f32[9,128]{1,0:T(8,128)S(1)}, f32[9,128]{1,0:T(8,128)S(1)}, u32[]{:S(2)}, u32[]{:S(2)}) collective-permute-start(f32[9,128]{1,0:T(8,128)S(1)} %get-tuple-element.53), channel_id=1, source_target_pairs={{2,0},{4,2},{6,4},{8,6},{10,8},{12,10},{14,12},{16,14},{18,16},{20... | collective-permute-start | bytes 13832 | tf_op jit(solution)/shard_map/ppermute | solution.py:483
  12.3 1.8 %collective-permute-start.2 = (f32[9,128]{1,0:T(8,128)S(1)}, f32[9,128]{1,0:T(8,128)S(1)}, u32[]{:S(2)}, u32[]{:S(2)}) collective-permute-start(f32[9,128]{1,0:T(8,128)S(1)} %get-tuple-element.54), channel_id=1, source_target_pairs={{0,1},{1,0},{2,3},{3,2},{4,5},{5,4},{6,7},{7,6},{8,9},{9,8},{10,11... | collective-permute-start | bytes 13832 | tf_op jit(solution)/shard_map/ppermute | solution.py:484
  15.6 8.5 %collective-permute-start.3 = (f32[64,128]{1,0:T(8,128)S(1)}, f32[64,128]{1,0:T(8,128)S(1)}, u32[]{:S(2)}, u32[]{:S(2)}) collective-permute-start(f32[64,128]{1,0:T(8,128)S(1)} %get-tuple-element.63), channel_id=1, source_target_pairs={{0,2},{2,4},{4,6},{6,8},{8,10},{10,12},{12,14},{14,16},{16,18},{18... | collective-permute-start | bytes 98312 | tf_op jit(solution)/shard_map/ppermute | solution.py:481
  18.9 5.1 %collective-permute-start.4 = (f32[64,128]{1,0:T(8,128)S(1)}, f32[64,128]{1,0:T(8,128)S(1)}, u32[]{:S(2)}, u32[]{:S(2)}) collective-permute-start(f32[64,128]{1,0:T(8,128)S(1)} %get-tuple-element.64), channel_id=1, source_target_pairs={{2,0},{4,2},{6,4},{8,6},{10,8},{12,10},{14,12},{16,14},{18,16},{20... | collective-permute-start | bytes 98312 | tf_op jit(solution)/shard_map/ppermute | solution.py:483
  22.5 2.3 %collective-permute-start.5 = (f32[64,128]{1,0:T(8,128)S(1)}, f32[64,128]{1,0:T(8,128)S(1)}, u32[]{:S(2)}, u32[]{:S(2)}) collective-permute-start(f32[64,128]{1,0:T(8,128)S(1)} %get-tuple-element.65), channel_id=1, source_target_pairs={{0,1},{1,0},{2,3},{3,2},{4,5},{5,4},{6,7},{7,6},{8,9},{9,8},{10,11... | collective-permute-start | bytes 98312 | tf_op jit(solution)/shard_map/ppermute | solution.py:484

commit v3 on v2

--- a/solution.py
+++ b/solution.py
@@ -10,22 +10,24 @@
 LANES = 128
 VMEM = pl.BlockSpec(memory_space=pltpu.VMEM)
 HBM = pl.BlockSpec(memory_space=pltpu.HBM)
-UNROLL = 2
 WIDTH = 64
 EDGE = 4
+SUM_REACH = 2
 LIMIT = 24 * 1024 * 1024
+
+
+EDGES = ((0, 1), (1, 2), (0, 2), (0, 3), (1, 3), (2, 3))
 
 
 def shape_table():
     near = 0.5854101966249685
     far = 0.1381966011250105
-    edge_pairs = ((0, 1), (1, 2), (0, 2), (0, 3), (1, 3), (2, 3))
     table_rows = []
     for corner in range(4):
         barycentric = [far, far, far, far]
         barycentric[corner] = near
         values = [b * (2.0 * b - 1.0) for b in barycentric]
-        values = values + [4.0 * barycentric[a] * barycentric[b] for a, b in edge_pairs]
+        values = values + [4.0 * barycentric[a] * barycentric[b] for a, b in EDGES]
         table_rows.append(values)
     return np.array(table_rows, np.float32)
 
@@ -109,8 +111,8 @@
     )(coords, disp, send, conn)
 
 
-def at_edge():
-    return lax.rem(lax.axis_index("dom"), EDGE) == 0
+def near_edge(reach):
+    return lax.rem(lax.axis_index("dom"), EDGE) < reach
 
 
 def gather_work(table_ref, ninth_ref, conn_ref, far, near, sems):
@@ -138,25 +140,27 @@
 
 
 def early_gather_kernel(*refs):
-    held, outs, sems = refs[7:9], refs[15:17], refs[17]
+    count = (len(refs) - 14) // 2
+    held, sems = refs[7:7 + count], refs[-1]
+    near, outs = refs[7 + count:13 + count], refs[13 + count:13 + 2 * count]
     for source, target in zip(held, outs):
         target[...] = source[...]
 
-    @pl.when(at_edge())
+    @pl.when(near_edge(1))
     def _():
-        gather_work(*refs[0:3], refs[3:7], refs[9:15], sems)
+        gather_work(*refs[0:3], refs[3:7], near, sems)
 
 
 def late_gather_kernel(*refs):
     sems = refs[19]
     done, near = refs[7:13], refs[13:19]
 
-    @pl.when(at_edge())
+    @pl.when(near_edge(1))
     def _():
         for source, target in zip(done, near):
             target[...] = source[...]
 
-    @pl.when(jnp.logical_not(at_edge()))
+    @pl.when(jnp.logical_not(near_edge(1)))
     def _():
         gather_work(*refs[0:3], refs[3:7], near, sems)
 
@@ -189,51 +193,52 @@
         ninth_ref[side:side + 1, :] = ref[8:9, :]
     sub = lax.broadcasted_iota(jnp.int32, (8, LANES), 0)
     groups = conn_ref.shape[1] // LANES
-
-    def group(block, slot):
-        lanes = pl.ds(pl.multiple_of(block * LANES, LANES), LANES)
-        corners, edges = [], []
+    ends = SHAPE[0, 1], SHAPE[0, 0] - SHAPE[0, 1]
+    mids = SHAPE[0, 5], SHAPE[0, 4] - SHAPE[0, 5]
+
+    def group(block):
+        lanes = slice(block * LANES, (block + 1) * LANES)
+        nodes = []
         for node in range(10):
             index = rows8(conn_ref, node, lanes)
             low, high = index & 127, index >> 7
             first = first_ref[node, :, lanes]
             for side in range(3):
                 first = jnp.where(high == first_halo + side, lane_gather(halos[side][0:8, :], low), first)
-            (corners if node < 4 else edges).append(first)
-            full_ref[slot, node, 0:8, :] = first
+            nodes.append(first)
+            full_ref[block, node, 0:8, :] = first
             last = jnp.where(high == sub + first_halo, lane_gather(ninth_ref[...], low), 0.0)
-            full_ref[slot, node, 8:16, :] = jnp.where(sub == 3, rows8(last_ref, node, lanes), last)
-        totals = [[jnp.zeros((8, LANES), jnp.float32) for _ in range(3)] for _ in range(2)]
+            full_ref[block, node, 8:16, :] = last
+        totals = [[None] * 3 for _ in range(2)]
         for node in range(10):
             for comp in range(3):
                 oper = oper_ref[3 * node + comp, :, lanes].astype(jnp.float32)
                 for step in range(2):
                     row = 3 + 3 * step + comp
-                    value = jnp.broadcast_to(full_ref[slot, node, row:row + 1, :], (8, LANES))
+                    value = rows8(full_ref.at[block, node], row, slice(0, LANES))
                     if row == 8:
-                        for extra in (9, 10, 11):
-                            value = value + jnp.broadcast_to(full_ref[slot, node, extra:extra + 1, :], (8, LANES))
+                        value = value + rows8(last_ref, node, lanes)
+                        for extra in (9, 10):
+                            value = value + rows8(full_ref.at[block, node], extra, slice(0, LANES))
                     for part in range(3):
-                        totals[step][part] = totals[step][part] + oper[8 * part:8 * part + 8] * value
-        for step in range(2):
-            for part in range(3):
-                row = 24 * step + 8 * part
-                blk_ref[row:row + 8, lanes] = totals[step][part]
+                        term = oper[8 * part:8 * part + 8] * value
+                        total = totals[step][part]
+                        totals[step][part] = term if total is None else total + term
+        pieces = totals[0] + totals[1]
+        shared = (nodes[0] + nodes[1] + nodes[2] + nodes[3]) * ends[0] + (
+            nodes[4] + nodes[5] + nodes[6] + nodes[7] + nodes[8] + nodes[9]
+        ) * mids[0]
         points = []
         for quad in range(4):
-            total = corners[0] * SHAPE[quad, 0]
-            for node in range(1, 10):
-                total = total + (corners + edges)[node] * SHAPE[quad, node]
-            points.append(total)
-        blk_ref[48:56, lanes] = jnp.where(sub < 4, points[0], pltpu.roll(points[1], 4, 0))
-        blk_ref[56:64, lanes] = jnp.where(sub < 4, points[2], pltpu.roll(points[3], 4, 0))
-
-    def pair(block, carry):
-        for slot in range(UNROLL):
-            group(block * UNROLL + slot, slot)
-        return carry
-
-    lax.fori_loop(0, groups // UNROLL, pair, 0)
+            a, b, c = [4 + k for k, pair in enumerate(EDGES) if quad in pair]
+            points.append(shared + nodes[quad] * ends[1] + (nodes[a] + nodes[b] + nodes[c]) * mids[1])
+        pieces.append(jnp.where(sub < 4, points[0], pltpu.roll(points[1], 4, 0)))
+        pieces.append(jnp.where(sub < 4, points[2], pltpu.roll(points[3], 4, 0)))
+        for part, piece in enumerate(pieces):
+            blk_ref[8 * part:8 * part + 8, lanes] = piece
+
+    for block in range(groups):
+        group(block)
     for side, out_ref in enumerate((prev_ref, next_ref, other_ref)):
         index = jnp.broadcast_to(send_ref[side], (8, LANES))
         low, high = index & 127, index >> 7
@@ -260,7 +265,7 @@
         out_specs=(VMEM,) * 4,
         scratch_shapes=[
             pltpu.VMEM((8, LANES), jnp.float32),
-            pltpu.VMEM((UNROLL, 10, 16, LANES), jnp.float32),
+            pltpu.VMEM((elems // LANES, 10, 16, LANES), jnp.float32),
         ],
         compiler_params=pltpu.CompilerParams(vmem_limit_bytes=LIMIT),
         name="make_blocks",
@@ -294,17 +299,17 @@
 
 
 def summed_over(moments, weights, weight_dim):
-    total = None
-    rest = moments
+    rows = moments.shape[0]
+    pieces, rest = [], moments
     for part in range(3):
-        piece = rest.astype(jnp.bfloat16)
+        pieces.append(rest.astype(jnp.bfloat16))
         if part < 2:
-            rest = rest - piece.astype(jnp.float32)
-        term = lax.dot_general(
-            piece, weights, (((1,), (weight_dim,)), ((), ())), preferred_element_type=jnp.float32
-        )
-        total = term if total is None else total + term
-    return total
+            rest = rest - pieces[part].astype(jnp.float32)
+    total = lax.dot_general(
+        jnp.concatenate(pieces, axis=0), weights, (((1,), (weight_dim,)), ((), ())),
+        preferred_element_type=jnp.float32,
+    )
+    return (total[2 * rows:] + total[rows:2 * rows]) + total[0:rows]
 
 
 def sum_work(
@@ -364,24 +369,25 @@
     sum_ref[...] = summed_over(moment_ref[...], weight_ref[...], 1)
 
 
-def early_sum_kernel(
-    list_ref, count_ref, blk_ref, prev_ref, other_ref, sum_ref, halo_ref, prev_out, other_out, *scratch
-):
-    prev_out[...] = prev_ref[...]
-    other_out[...] = other_ref[...]
-
-    @pl.when(at_edge())
+def early_sum_kernel(list_ref, count_ref, blk_ref, *refs):
+    count = (len(refs) - 6) // 2
+    sum_ref, halo_ref = refs[count:count + 2]
+    scratch = refs[2 + 2 * count:]
+    for source, target in zip(refs[0:count], refs[count + 2:2 * count + 2]):
+        target[...] = source[...]
+
+    @pl.when(near_edge(SUM_REACH))
     def _():
         sum_work(list_ref, count_ref, blk_ref, sum_ref, halo_ref, *scratch)
 
 
 def late_sum_kernel(list_ref, count_ref, blk_ref, sum_in, halo_in, sum_ref, halo_ref, *scratch):
-    @pl.when(at_edge())
+    @pl.when(near_edge(SUM_REACH))
     def _():
         sum_ref[...] = sum_in[...]
         halo_ref[...] = halo_in[...]
 
-    @pl.when(jnp.logical_not(at_edge()))
+    @pl.when(jnp.logical_not(near_edge(SUM_REACH)))
     def _():
         sum_work(list_ref, count_ref, blk_ref, sum_ref, halo_ref, *scratch)
 

time: 25.9 us -> 25.6 us (0.988)
  Pallas kernels: 8.78 us -> 8.35 us
  transfers between devices with their start and end apart: 6 -> 6, of which waited for: 2 -> 2; matrix products, arithmetic and copies ran while one was open for 0% -> 0% of each run, Pallas kernels for 21% -> 20%
where the time goes in v3:
time: 25.6 us; the launch traced here: 25.5 us
  starting transfers between devices  15.6 us (61%)
  Pallas kernels  8.35 us (33%)
  waiting for transfers between devices  1.45 us (6%)
    ppermute x2, starting transfers between devices, exchange(): from_next = lax.ppermute(to_prev, 'dom', down)  11 us
    pallas_call x2, Pallas kernels, own_sums(): pl.pallas_call(late_sum_kernel if held is None else early_sum_kernel, out...  3.1 us
    ppermute x2, starting transfers between devices, exchange(): from_other = lax.ppermute(to_other, 'slab', swap)  2.43 us
    ppermute x2, starting transfers between devices, exchange(): from_prev = lax.ppermute(to_next, 'dom', up)  2.2 us
    pallas_call x2, Pallas kernels, own_gather(): pl.pallas_call(late_gather_kernel if held is None else early_gather_kerne...  2.12 us
    ppermute x2, waiting for transfers between devices, exchange(): from_other = lax.ppermute(to_other, 'slab', swap)  1.44 us
    pallas_call x1, Pallas kernels, make_blocks(): pl.pallas_call(kernel, out_shape=(jax.ShapeDtypeStruct((64, elems), jnp.f...  1.26 us
    pallas_call x1, Pallas kernels, node_pick(): pl.pallas_call(node_pick_kernel, out_shape=(out, out, out, jax.ShapeDtype...  0.97 us
  transfers between devices with their start and end apart: 6, of which 2 were waited for; matrix products, arithmetic and copies ran while one was open for 0% of the time, Pallas kernels for 20%

profile of v3, /device:TPU:1, one launch (start us, length us, event | category | flops | bytes accessed | tf_op | source)
XLA Modules:
  0.0 25.5 jit_solution(10230139120141323299)
XLA Ops:
  0.0 1.0 %node_pick.1 = (f32[9,128]{1,0:T(8,128)S(1)}, f32[9,128]{1,0:T(8,128)S(1)}, f32[9,128]{1,0:T(8,128)S(1)}, f32[11,8,128]{2,1,0:T(8,128)S(1)}, f32[16,128]{1,0:T(8...) custom-call(f32[3,1408]{1,0:T(4,128)} %coords_hbm.1, f32[6,1408]{1,0:T(8,128)} %disp_hbm.1, ...), custom_call_target="tpu_custom_call" | custom-call | tf_op jit(solution)/shard_map/node_pick/pallas_call | solution.py:93
  1.0 2.1 %collective-permute-start = (f32[9,128]{1,0:T(8,128)S(1)}, f32[9,128]{1,0:T(8,128)S(1)}, u32[]{:S(2)}, u32[]{:S(2)}) collective-permute-start(f32[9,128]{1,0:T(8,128)S(1)} %get-tuple-element.52), channel_id=1, source_target_pairs={{0,2},{2,4},{4,6},{6,8},{8,10},{10,12},{12,14},{14,16},{16,18},{18... | collective-permute-start | bytes 13832 | tf_op jit(solution)/shard_map/ppermute | solution.py:487
  3.1 2.0 %early_gather.1 = (f32[10,8,1024]{2,1,0:T(8,128)S(1)}, f32[10,1024]{1,0:T(8,128)S(1)}, bf16[30,24,1024]{2,1,0:T(8,128)(2,1)S(1)}, s32[192,128]{1,0:T(8,128)S(1)}...) custom-call(f32[11,8,128]{2,1,0:T(8,128)S(1)} %get-tuple-element.36.refs_0_, ...), custom_call_target="tpu_custom_call" | custom-call | flops 20000000 | bytes 4000000 | tf_op jit(solution)/shard_map/early_gather/pallas_call | solution.py:175
  5.1 7.2 %collective-permute-start.1 = (f32[9,128]{1,0:T(8,128)S(1)}, f32[9,128]{1,0:T(8,128)S(1)}, u32[]{:S(2)}, u32[]{:S(2)}) collective-permute-start(f32[9,128]{1,0:T(8,128)S(1)} %get-tuple-element.53), channel_id=1, source_target_pairs={{2,0},{4,2},{6,4},{8,6},{10,8},{12,10},{14,12},{16,14},{18,16},{20... | collective-permute-start | bytes 13832 | tf_op jit(solution)/shard_map/ppermute | solution.py:489
  12.3 1.0 %collective-permute-start.2 = (f32[9,128]{1,0:T(8,128)S(1)}, f32[9,128]{1,0:T(8,128)S(1)}, u32[]{:S(2)}, u32[]{:S(2)}) collective-permute-start(f32[9,128]{1,0:T(8,128)S(1)} %get-tuple-element.54), channel_id=1, source_target_pairs={{0,1},{1,0},{2,3},{3,2},{4,5},{5,4},{6,7},{7,6},{8,9},{9,8},{10,11... | collective-permute-start | bytes 13832 | tf_op jit(solution)/shard_map/ppermute | solution.py:490
  13.2 0.2 late_gather.1
  13.4 0.0 collective-permute-done.refs_4_
  13.4 0.0 collective-permute-done.1.refs_5_
  13.4 0.6 %collective-permute-done.2.refs_6_ = f32[9,128]{1,0:T(8,128)S(1)} collective-permute-done((f32[9,128]{1,0:T(8,128)S(1)}, f32[9,128]{1,0:T(8,128)S(1)}, u32[]{:S(2)}, u32[]{:S(2)}) %collective-permute-start.2) | collective-permute-done | bytes 4640 | tf_op jit(solution)/shard_map/ppermute | solution.py:490
  14.0 1.3 %make_blocks.1 = (f32[64,1024]{1,0:T(8,128)S(1)}, f32[64,128]{1,0:T(8,128)S(1)}, f32[64,128]{1,0:T(8,128)S(1)}, f32[64,128]{1,0:T(8,128)S(1)}) custom-call(f32[10,8,1024]{2,1,0:T(8,128)S(1)} %get-tuple-element.49.refs_0_, f32[10,1024]{1,0:T(8,128)S(1)} %get-tuple-element.50.refs_1_, s32[10,1024]{1,0:T(8,128)S(1)} %get-tuple-element.38.refs_2_, ...), custom_call_target="tpu_custom_call" | custom-call | tf_op jit(solution)/shard_map/make_blocks/pallas_call | solution.py:261
  15.3 0.1 collective-permute-start.3
  15.4 3.1 %early_sums.1 = (f32[96,192]{1,0:T(8,128)S(1)}, bf16[384,192]{1,0:T(8,128)(2,1)S(1)}, f32[64,128]{1,0:T(8,128)S(1)}, f32[64,128]{1,0:T(8,128)S(1)}) custom-call(s32[192,128]{1,0:T(8,128)S(1)} %get-tuple-element.47.list_ref, s32[1,192]{1,0:T(1,128)S(1)} %get-tuple-element.48.count_ref, f32[64,1024]{1,0:T(8,128)S(1)} %get-tuple-element.56.blk_ref, ...), custom_call_target="tpu_custom_call" | custom-call | flops 40000000 | bytes 8000000 | tf_op jit(solution)/shard_map/early_sums/pallas_call | solution.py:405
  18.5 3.8 %collective-permute-start.4 = (f32[64,128]{1,0:T(8,128)S(1)}, f32[64,128]{1,0:T(8,128)S(1)}, u32[]{:S(2)}, u32[]{:S(2)}) collective-permute-start(f32[64,128]{1,0:T(8,128)S(1)} %get-tuple-element.64), channel_id=1, source_target_pairs={{2,0},{4,2},{6,4},{8,6},{10,8},{12,10},{14,12},{16,14},{18,16},{20... | collective-permute-start | bytes 98312 | tf_op jit(solution)/shard_map/ppermute | solution.py:489
  22.3 1.5 %collective-permute-start.5 = (f32[64,128]{1,0:T(8,128)S(1)}, f32[64,128]{1,0:T(8,128)S(1)}, u32[]{:S(2)}, u32[]{:S(2)}) collective-permute-start(f32[64,128]{1,0:T(8,128)S(1)} %get-tuple-element.65), channel_id=1, source_target_pairs={{0,1},{1,0},{2,3},{3,2},{4,5},{5,4},{6,7},{7,6},{8,9},{9,8},{10,11... | collective-permute-start | bytes 98312 | tf_op jit(solution)/shard_map/ppermute | solution.py:490
  23.8 0.0 collective-permute-done.3.h0_ref
  23.8 0.0 collective-permute-done.4.h1_ref
  23.8 0.8 %collective-permute-done.5.h2_ref = f32[64,128]{1,0:T(8,128)S(1)} collective-permute-done((f32[64,128]{1,0:T(8,128)S(1)}, f32[64,128]{1,0:T(8,128)S(1)}, u32[]{:S(2)}, u32[]{:S(2)}) %collective-permute-start.5) | collective-permute-done | bytes 32800 | tf_op jit(solution)/shard_map/ppermute | solution.py:490
  24.6 0.9 %fit.1 = f32[12,192]{1,0:T(8,128)} custom-call(f32[96,192]{1,0:T(8,128)S(1)} %get-tuple-element.61.sum_ref, bf16[384,192]{1,0:T(8,128)(2,1)S(1)} %get-tuple-element.62.weight_ref, f32[64,128]{1,0:T(8,128)S(1)} %collective-permute-done.3.h0_ref, f32[64,128]{1,0:T(8,128)S(1)} %collective-permute-done.4.h1_ref, f32[64,128]{1,0:T(8,128)S(1)} %collective-permute-done.5.h2_ref, ...), custom_call_target="tpu_custom_call" | custom-call | tf_op jit(solution)/shard_map/fit/pallas_call | solution.py:468
  (1 shorter events, 0.0 us)
Async XLA Ops:
  1.0 12.4 %collective-permute-start = (f32[9,128]{1,0:T(8,128)S(1)}, f32[9,128]{1,0:T(8,128)S(1)}, u32[]{:S(2)}, u32[]{:S(2)}) collective-permute-start(f32[9,128]{1,0:T(8,128)S(1)} %get-tuple-element.52), channel_id=1, source_target_pairs={{0,2},{2,4},{4,6},{6,8},{8,10},{10,12},{12,14},{14,16},{16,18},{18... | collective-permute-start | bytes 13832 | tf_op jit(solution)/shard_map/ppermute | solution.py:487
  5.1 8.3 %collective-permute-start.1 = (f32[9,128]{1,0:T(8,128)S(1)}, f32[9,128]{1,0:T(8,128)S(1)}, u32[]{:S(2)}, u32[]{:S(2)}) collective-permute-start(f32[9,128]{1,0:T(8,128)S(1)} %get-tuple-element.53), channel_id=1, source_target_pairs={{2,0},{4,2},{6,4},{8,6},{10,8},{12,10},{14,12},{16,14},{18,16},{20... | collective-permute-start | bytes 13832 | tf_op jit(solution)/shard_map/ppermute | solution.py:489
  12.3 1.8 %collective-permute-start.2 = (f32[9,128]{1,0:T(8,128)S(1)}, f32[9,128]{1,0:T(8,128)S(1)}, u32[]{:S(2)}, u32[]{:S(2)}) collective-permute-start(f32[9,128]{1,0:T(8,128)S(1)} %get-tuple-element.54), channel_id=1, source_target_pairs={{0,1},{1,0},{2,3},{3,2},{4,5},{5,4},{6,7},{7,6},{8,9},{9,8},{10,11... | collective-permute-start | bytes 13832 | tf_op jit(solution)/shard_map/ppermute | solution.py:490
  15.3 8.5 %collective-permute-start.3 = (f32[64,128]{1,0:T(8,128)S(1)}, f32[64,128]{1,0:T(8,128)S(1)}, u32[]{:S(2)}, u32[]{:S(2)}) collective-permute-start(f32[64,128]{1,0:T(8,128)S(1)} %get-tuple-element.63), channel_id=1, source_target_pairs={{0,2},{2,4},{4,6},{6,8},{8,10},{10,12},{12,14},{14,16},{16,18},{18... | collective-permute-start | bytes 98312 | tf_op jit(solution)/shard_map/ppermute | solution.py:487
  18.5 5.3 %collective-permute-start.4 = (f32[64,128]{1,0:T(8,128)S(1)}, f32[64,128]{1,0:T(8,128)S(1)}, u32[]{:S(2)}, u32[]{:S(2)}) collective-permute-start(f32[64,128]{1,0:T(8,128)S(1)} %get-tuple-element.64), channel_id=1, source_target_pairs={{2,0},{4,2},{6,4},{8,6},{10,8},{12,10},{14,12},{16,14},{18,16},{20... | collective-permute-start | bytes 98312 | tf_op jit(solution)/shard_map/ppermute | solution.py:489
  22.3 2.3 %collective-permute-start.5 = (f32[64,128]{1,0:T(8,128)S(1)}, f32[64,128]{1,0:T(8,128)S(1)}, u32[]{:S(2)}, u32[]{:S(2)}) collective-permute-start(f32[64,128]{1,0:T(8,128)S(1)} %get-tuple-element.65), channel_id=1, source_target_pairs={{0,1},{1,0},{2,3},{3,2},{4,5},{5,4},{6,7},{7,6},{8,9},{9,8},{10,11... | collective-permute-start | bytes 98312 | tf_op jit(solution)/shard_map/ppermute | solution.py:490

commit v4 on v3

--- a/solution.py
+++ b/solution.py
@@ -59,13 +59,11 @@
 
 
 def node_pick_kernel(
-    coords_hbm, disp_hbm, send_hbm, conn_hbm,
-    prev_ref, next_ref, other_ref, table_ref, ninth_ref, coords_ref, conn_ref,
+    coords_hbm, disp_hbm, send_hbm, prev_ref, next_ref, other_ref, table_ref, ninth_ref, coords_ref,
     disp_ref, send_ref, sems,
 ):
-    pairs = ((coords_hbm, coords_ref), (disp_hbm, disp_ref), (send_hbm, send_ref), (conn_hbm, conn_ref))
-    copies = start_all(pairs, sems)
-    for copy in copies[0:3]:
+    pairs = ((coords_hbm, coords_ref), (disp_hbm, disp_ref), (send_hbm, send_ref))
+    for copy in start_all(pairs, sems):
         copy.wait()
     sub = lax.broadcasted_iota(jnp.int32, (8, LANES), 0)
     chunks = table_ref.shape[0]
@@ -84,10 +82,9 @@
         out_ref[0:8, :] = first
         last = ninth_row(sub, ninth_ref, low, high, chunks)
         out_ref[8:9, :] = jnp.sum(last, axis=0, keepdims=True)
-    copies[3].wait()
-
-
-def node_pick(coords, disp, send, conn):
+
+
+def node_pick(coords, disp, send):
     out = jax.ShapeDtypeStruct((9, LANES), jnp.float32)
     chunks = coords.shape[1] // LANES
     return pl.pallas_call(
@@ -97,27 +94,27 @@
             jax.ShapeDtypeStruct((chunks, 8, LANES), jnp.float32),
             jax.ShapeDtypeStruct((16, LANES), jnp.float32),
             jax.ShapeDtypeStruct(coords.shape, coords.dtype),
-            jax.ShapeDtypeStruct(conn.shape, conn.dtype),
         ),
-        in_specs=[HBM] * 4,
-        out_specs=(VMEM,) * 7,
+        in_specs=[HBM] * 3,
+        out_specs=(VMEM,) * 6,
         scratch_shapes=[
             pltpu.VMEM(disp.shape, disp.dtype),
             pltpu.VMEM(send.shape, send.dtype),
-            pltpu.SemaphoreType.DMA((4,)),
+            pltpu.SemaphoreType.DMA((3,)),
         ],
         compiler_params=pltpu.CompilerParams(vmem_limit_bytes=LIMIT),
         name="node_pick",
-    )(coords, disp, send, conn)
+    )(coords, disp, send)
 
 
 def near_edge(reach):
     return lax.rem(lax.axis_index("dom"), EDGE) < reach
 
 
-def gather_work(table_ref, ninth_ref, conn_ref, far, near, sems):
-    first_ref, last_ref = near[0:2]
-    copies = start_all(tuple(zip(far, near[2:6])), sems)
+def gather_work(table_ref, ninth_ref, far, near, sems):
+    first_ref, last_ref, conn_ref = near[0:3]
+    copies = start_all(tuple(zip(far, near[2:7])), sems)
+    copies[0].wait()
     sub = lax.broadcasted_iota(jnp.int32, (8, LANES), 0)
     chunks = table_ref.shape[0]
 
@@ -135,25 +132,25 @@
         return carry
 
     lax.fori_loop(0, conn_ref.shape[1] // LANES, group, 0)
-    for copy in copies:
+    for copy in copies[1:]:
         copy.wait()
 
 
 def early_gather_kernel(*refs):
-    count = (len(refs) - 14) // 2
+    count = (len(refs) - 15) // 2
     held, sems = refs[7:7 + count], refs[-1]
-    near, outs = refs[7 + count:13 + count], refs[13 + count:13 + 2 * count]
+    near, outs = refs[7 + count:14 + count], refs[14 + count:14 + 2 * count]
     for source, target in zip(held, outs):
         target[...] = source[...]
 
     @pl.when(near_edge(1))
     def _():
-        gather_work(*refs[0:3], refs[3:7], near, sems)
+        gather_work(*refs[0:2], refs[2:7], near, sems)
 
 
 def late_gather_kernel(*refs):
-    sems = refs[19]
-    done, near = refs[7:13], refs[13:19]
+    sems = refs[21]
+    done, near = refs[7:14], refs[14:21]
 
     @pl.when(near_edge(1))
     def _():
@@ -162,11 +159,11 @@
 
     @pl.when(jnp.logical_not(near_edge(1)))
     def _():
-        gather_work(*refs[0:3], refs[3:7], near, sems)
-
-
-def own_gather(table, ninth, conn, far, held=None, done=None):
-    elems = conn.shape[1]
+        gather_work(*refs[0:2], refs[2:7], near, sems)
+
+
+def own_gather(table, ninth, far, held=None, done=None):
+    elems = far[0].shape[1]
     outs = [jax.ShapeDtypeStruct((10, 8, elems), jnp.float32), jax.ShapeDtypeStruct((10, elems), jnp.float32)]
     outs = outs + [jax.ShapeDtypeStruct(x.shape, x.dtype) for x in far]
     extra = list(done) if held is None else list(held)
@@ -175,13 +172,13 @@
     return pl.pallas_call(
         late_gather_kernel if held is None else early_gather_kernel,
         out_shape=tuple(outs),
-        in_specs=[VMEM] * 3 + [HBM] * 4 + [VMEM] * len(extra),
+        in_specs=[VMEM] * 2 + [HBM] * 5 + [VMEM] * len(extra),
         out_specs=(VMEM,) * len(outs),
-        scratch_shapes=[pltpu.SemaphoreType.DMA((4,))],
+        scratch_shapes=[pltpu.SemaphoreType.DMA((5,))],
         compiler_params=pltpu.CompilerParams(vmem_limit_bytes=LIMIT),
         cost_estimate=pl.CostEstimate(flops=20000000, bytes_accessed=4000000, transcendentals=0),
         name="late_gather" if held is None else "early_gather",
-    )(table, ninth, conn, *far, *extra)
+    )(table, ninth, *far, *extra)
 
 
 def block_kernel(
@@ -499,10 +496,10 @@
     far = [pltpu.with_memory_space_constraint(x, pltpu.HBM) for x in (
         coords, disp, node_send, conn, oper, listed, patch_count, element_send
     )]
-    *picked, table, ninth, coords_near, conn_near = node_pick(*far[0:4])
-    own = (table, ninth, conn_near, far[4:8])
+    *picked, table, ninth, coords_near = node_pick(*far[0:3])
+    own = (table, ninth, far[3:8])
     halos, done = exchange(*picked, lambda held: own_gather(*own, held=held))
-    first, last, oper, listed, counts, send = own_gather(*own, done=done)
+    first, last, conn_near, oper, listed, counts, send = own_gather(*own, done=done)
     blk, *picked = make_blocks(first, last, conn_near, oper, halos, send, coords.shape[1] // LANES)
     own = (listed, counts, blk)
     halos, done = exchange(*picked, lambda held: own_sums(*own, held=held))

time: 25.6 us -> 25.7 us (level)
  Pallas kernels: 8.35 us -> 9.21 us
  starting transfers between devices: 15.6 us -> 14.8 us
    pallas_call x2, Pallas kernels: 2.12 us -> 2.98 us  [own_gather(): pl.pallas_call(late_gather_kernel if held is None else early_gather_kerne...]
    ppermute x2, starting transfers between devices: 11 us -> 10.2 us  [exchange(): from_next = lax.ppermute(to_prev, 'dom', down)]
  transfers between devices with their start and end apart: 6 -> 6, of which waited for: 2 -> 2; matrix products, arithmetic and copies ran while one was open for 0% -> 0% of each run, Pallas kernels for 20% -> 24%
where the time goes in v4:
time: 25.7 us; the launch traced here: 25.5 us
  starting transfers between devices  14.8 us (58%)
  Pallas kernels  9.21 us (36%)
  waiting for transfers between devices  1.44 us (6%)
    ppermute x2, starting transfers between devices, exchange(): from_next = lax.ppermute(to_prev, 'dom', down)  10.2 us
    pallas_call x2, Pallas kernels, own_sums(): pl.pallas_call(late_sum_kernel if held is None else early_sum_kernel, out...  3.11 us
    pallas_call x2, Pallas kernels, own_gather(): pl.pallas_call(late_gather_kernel if held is None else early_gather_kerne...  2.98 us
    ppermute x2, starting transfers between devices, exchange(): from_other = lax.ppermute(to_other, 'slab', swap)  2.43 us
    ppermute x2, starting transfers between devices, exchange(): from_prev = lax.ppermute(to_next, 'dom', up)  2.2 us
    ppermute x2, waiting for transfers between devices, exchange(): from_other = lax.ppermute(to_other, 'slab', swap)  1.43 us
    pallas_call x1, Pallas kernels, make_blocks(): pl.pallas_call(kernel, out_shape=(jax.ShapeDtypeStruct((64, elems), jnp.f...  1.26 us
    pallas_call x1, Pallas kernels, node_pick(): pl.pallas_call(node_pick_kernel, out_shape=(out, out, out, jax.ShapeDtype...  0.96 us
  transfers between devices with their start and end apart: 6, of which 2 were waited for; matrix products, arithmetic and copies ran while one was open for 0% of the time, Pallas kernels for 24%

profile of v4, /device:TPU:1, one launch (start us, length us, event | category | flops | bytes accessed | tf_op | source)
XLA Modules:
  0.0 25.5 jit_solution(8193928722609382535)
XLA Ops:
  0.0 1.0 %node_pick.1 = (f32[9,128]{1,0:T(8,128)S(1)}, f32[9,128]{1,0:T(8,128)S(1)}, f32[9,128]{1,0:T(8,128)S(1)}, f32[11,8,128]{2,1,0:T(8,128)S(1)}, f32[16,128]{1,0:T(8,128)S(1)}, /*index=5*/f32[3,1408]{1,0:T(4,128)S(1)}) custom-call(f32[3,1408]{1,0:T(4,128)} %coords_hbm.1, f32[6,1408]{1,0:T(8,128)} %disp_hbm.1, s32[3,1,128]{2,1,0:T(1,128)} %bitcast.10), custom_call_target="tpu_custom_call" | custom-call | tf_op jit(solution)/shard_map/node_pick/pallas_call | solution.py:90
  1.0 2.1 %collective-permute-start = (f32[9,128]{1,0:T(8,128)S(1)}, f32[9,128]{1,0:T(8,128)S(1)}, u32[]{:S(2)}, u32[]{:S(2)}) collective-permute-start(f32[9,128]{1,0:T(8,128)S(1)} %get-tuple-element.54), channel_id=1, source_target_pairs={{0,2},{2,4},{4,6},{6,8},{8,10},{10,12},{12,14},{14,16},{16,18},{18... | collective-permute-start | bytes 13832 | tf_op jit(solution)/shard_map/ppermute | solution.py:484
  3.1 2.8 %early_gather.1 = (f32[10,8,1024]{2,1,0:T(8,128)S(1)}, f32[10,1024]{1,0:T(8,128)S(1)}, s32[10,1024]{1,0:T(8,128)S(1)}, bf16[30,24,1024]{2,1,0:T(8,128)(2,1)S(1)}...) custom-call(f32[11,8,128]{2,1,0:T(8,128)S(1)} %get-tuple-element.37., ...), custom_call_target="tpu_custom_call" | custom-call | flops 20000000 | bytes 4000000 | tf_op jit(solution)/shard_map/early_gather/pallas_call | solution.py:172
  5.9 6.4 %collective-permute-start.1 = (f32[9,128]{1,0:T(8,128)S(1)}, f32[9,128]{1,0:T(8,128)S(1)}, u32[]{:S(2)}, u32[]{:S(2)}) collective-permute-start(f32[9,128]{1,0:T(8,128)S(1)} %get-tuple-element.55), channel_id=1, source_target_pairs={{2,0},{4,2},{6,4},{8,6},{10,8},{12,10},{14,12},{16,14},{18,16},{20... | collective-permute-start | bytes 13832 | tf_op jit(solution)/shard_map/ppermute | solution.py:486
  12.3 1.0 %collective-permute-start.2 = (f32[9,128]{1,0:T(8,128)S(1)}, f32[9,128]{1,0:T(8,128)S(1)}, u32[]{:S(2)}, u32[]{:S(2)}) collective-permute-start(f32[9,128]{1,0:T(8,128)S(1)} %get-tuple-element.56), channel_id=1, source_target_pairs={{0,1},{1,0},{2,3},{3,2},{4,5},{5,4},{6,7},{7,6},{8,9},{9,8},{10,11... | collective-permute-start | bytes 13832 | tf_op jit(solution)/shard_map/ppermute | solution.py:487
  13.2 0.2 late_gather.1
  13.4 0.0 collective-permute-done.refs_4_
  13.4 0.0 collective-permute-done.1.refs_5_
  13.4 0.6 %collective-permute-done.2.refs_6_ = f32[9,128]{1,0:T(8,128)S(1)} collective-permute-done((f32[9,128]{1,0:T(8,128)S(1)}, f32[9,128]{1,0:T(8,128)S(1)}, u32[]{:S(2)}, u32[]{:S(2)}) %collective-permute-start.2) | collective-permute-done | bytes 4640 | tf_op jit(solution)/shard_map/ppermute | solution.py:487
  14.0 1.3 %make_blocks.1 = (f32[64,1024]{1,0:T(8,128)S(1)}, f32[64,128]{1,0:T(8,128)S(1)}, f32[64,128]{1,0:T(8,128)S(1)}, f32[64,128]{1,0:T(8,128)S(1)}) custom-call(f32[10,8,1024]{2,1,0:T(8,128)S(1)} %get-tuple-element.50.refs_0_, f32[10,1024]{1,0:T(8,128)S(1)} %get-tuple-element.51.refs_1_, s32[10,1024]{1,0:T(8,128)S(1)} %get-tuple-element.52.refs_2_, ...), custom_call_target="tpu_custom_call" | custom-call | tf_op jit(solution)/shard_map/make_blocks/pallas_call | solution.py:258
  15.3 0.1 collective-permute-start.3
  15.4 3.1 %early_sums.1 = (f32[96,192]{1,0:T(8,128)S(1)}, bf16[384,192]{1,0:T(8,128)(2,1)S(1)}, f32[64,128]{1,0:T(8,128)S(1)}, f32[64,128]{1,0:T(8,128)S(1)}) custom-call(s32[192,128]{1,0:T(8,128)S(1)} %get-tuple-element.48.list_ref, s32[1,192]{1,0:T(1,128)S(1)} %get-tuple-element.49.count_ref, f32[64,1024]{1,0:T(8,128)S(1)} %get-tuple-element.58.blk_ref, ...), custom_call_target="tpu_custom_call" | custom-call | flops 40000000 | bytes 8000000 | tf_op jit(solution)/shard_map/early_sums/pallas_call | solution.py:402
  18.5 3.8 %collective-permute-start.4 = (f32[64,128]{1,0:T(8,128)S(1)}, f32[64,128]{1,0:T(8,128)S(1)}, u32[]{:S(2)}, u32[]{:S(2)}) collective-permute-start(f32[64,128]{1,0:T(8,128)S(1)} %get-tuple-element.66), channel_id=1, source_target_pairs={{2,0},{4,2},{6,4},{8,6},{10,8},{12,10},{14,12},{16,14},{18,16},{20... | collective-permute-start | bytes 98312 | tf_op jit(solution)/shard_map/ppermute | solution.py:486
  22.3 1.5 %collective-permute-start.5 = (f32[64,128]{1,0:T(8,128)S(1)}, f32[64,128]{1,0:T(8,128)S(1)}, u32[]{:S(2)}, u32[]{:S(2)}) collective-permute-start(f32[64,128]{1,0:T(8,128)S(1)} %get-tuple-element.67), channel_id=1, source_target_pairs={{0,1},{1,0},{2,3},{3,2},{4,5},{5,4},{6,7},{7,6},{8,9},{9,8},{10,11... | collective-permute-start | bytes 98312 | tf_op jit(solution)/shard_map/ppermute | solution.py:487
  23.8 0.0 collective-permute-done.3.h0_ref
  23.8 0.0 collective-permute-done.4.h1_ref
  23.8 0.8 %collective-permute-done.5.h2_ref = f32[64,128]{1,0:T(8,128)S(1)} collective-permute-done((f32[64,128]{1,0:T(8,128)S(1)}, f32[64,128]{1,0:T(8,128)S(1)}, u32[]{:S(2)}, u32[]{:S(2)}) %collective-permute-start.5) | collective-permute-done | bytes 32800 | tf_op jit(solution)/shard_map/ppermute | solution.py:487
  24.6 0.9 %fit.1 = f32[12,192]{1,0:T(8,128)} custom-call(f32[96,192]{1,0:T(8,128)S(1)} %get-tuple-element.63.sum_ref, bf16[384,192]{1,0:T(8,128)(2,1)S(1)} %get-tuple-element.64.weight_ref, f32[64,128]{1,0:T(8,128)S(1)} %collective-permute-done.3.h0_ref, f32[64,128]{1,0:T(8,128)S(1)} %collective-permute-done.4.h1_ref, f32[64,128]{1,0:T(8,128)S(1)} %collective-permute-done.5.h2_ref, ...), custom_call_target="tpu_custom_call" | custom-call | tf_op jit(solution)/shard_map/fit/pallas_call | solution.py:465
  (1 shorter events, 0.0 us)
Async XLA Ops:
  1.0 12.4 %collective-permute-start = (f32[9,128]{1,0:T(8,128)S(1)}, f32[9,128]{1,0:T(8,128)S(1)}, u32[]{:S(2)}, u32[]{:S(2)}) collective-permute-start(f32[9,128]{1,0:T(8,128)S(1)} %get-tuple-element.54), channel_id=1, source_target_pairs={{0,2},{2,4},{4,6},{6,8},{8,10},{10,12},{12,14},{14,16},{16,18},{18... | collective-permute-start | bytes 13832 | tf_op jit(solution)/shard_map/ppermute | solution.py:484
  5.9 7.5 %collective-permute-start.1 = (f32[9,128]{1,0:T(8,128)S(1)}, f32[9,128]{1,0:T(8,128)S(1)}, u32[]{:S(2)}, u32[]{:S(2)}) collective-permute-start(f32[9,128]{1,0:T(8,128)S(1)} %get-tuple-element.55), channel_id=1, source_target_pairs={{2,0},{4,2},{6,4},{8,6},{10,8},{12,10},{14,12},{16,14},{18,16},{20... | collective-permute-start | bytes 13832 | tf_op jit(solution)/shard_map/ppermute | solution.py:486
  12.3 1.8 %collective-permute-start.2 = (f32[9,128]{1,0:T(8,128)S(1)}, f32[9,128]{1,0:T(8,128)S(1)}, u32[]{:S(2)}, u32[]{:S(2)}) collective-permute-start(f32[9,128]{1,0:T(8,128)S(1)} %get-tuple-element.56), channel_id=1, source_target_pairs={{0,1},{1,0},{2,3},{3,2},{4,5},{5,4},{6,7},{7,6},{8,9},{9,8},{10,11... | collective-permute-start | bytes 13832 | tf_op jit(solution)/shard_map/ppermute | solution.py:487
  15.3 8.5 %collective-permute-start.3 = (f32[64,128]{1,0:T(8,128)S(1)}, f32[64,128]{1,0:T(8,128)S(1)}, u32[]{:S(2)}, u32[]{:S(2)}) collective-permute-start(f32[64,128]{1,0:T(8,128)S(1)} %get-tuple-element.65), channel_id=1, source_target_pairs={{0,2},{2,4},{4,6},{6,8},{8,10},{10,12},{12,14},{14,16},{16,18},{18... | collective-permute-start | bytes 98312 | tf_op jit(solution)/shard_map/ppermute | solution.py:484
  18.5 5.3 %collective-permute-start.4 = (f32[64,128]{1,0:T(8,128)S(1)}, f32[64,128]{1,0:T(8,128)S(1)}, u32[]{:S(2)}, u32[]{:S(2)}) collective-permute-start(f32[64,128]{1,0:T(8,128)S(1)} %get-tuple-element.66), channel_id=1, source_target_pairs={{2,0},{4,2},{6,4},{8,6},{10,8},{12,10},{14,12},{16,14},{18,16},{20... | collective-permute-start | bytes 98312 | tf_op jit(solution)/shard_map/ppermute | solution.py:486
  22.3 2.3 %collective-permute-start.5 = (f32[64,128]{1,0:T(8,128)S(1)}, f32[64,128]{1,0:T(8,128)S(1)}, u32[]{:S(2)}, u32[]{:S(2)}) collective-permute-start(f32[64,128]{1,0:T(8,128)S(1)} %get-tuple-element.67), channel_id=1, source_target_pairs={{0,1},{1,0},{2,3},{3,2},{4,5},{5,4},{6,7},{7,6},{8,9},{9,8},{10,11... | collective-permute-start | bytes 98312 | tf_op jit(solution)/shard_map/ppermute | solution.py:487

commit v5 on v3

--- a/solution.py
+++ b/solution.py
@@ -12,7 +12,8 @@
 HBM = pl.BlockSpec(memory_space=pltpu.HBM)
 WIDTH = 64
 EDGE = 4
-SUM_REACH = 2
+HOLD = (True, False)
+SUM_REACH = 1
 LIMIT = 24 * 1024 * 1024
 
 
@@ -479,13 +480,16 @@
     )(sums, weights, *halos, coords, counts)
 
 
-def exchange(to_prev, to_next, to_other, early):
+def exchange(to_prev, to_next, to_other, early, hold):
     count = lax.axis_size("dom")
     up = [(i, (i + 1) % count) for i in range(count)]
     down = [(j, i) for i, j in up]
     swap = [(0, 1), (1, 0)]
     from_prev = lax.ppermute(to_next, "dom", up)
-    *done, to_prev, to_other = early((to_prev, to_other))
+    if hold:
+        *done, to_prev, to_other = early((to_prev, to_other))
+    else:
+        *done, to_prev = early((to_prev,))
     from_next = lax.ppermute(to_prev, "dom", down)
     from_other = lax.ppermute(to_other, "slab", swap)
     return (from_prev, from_next, from_other), done
@@ -501,11 +505,11 @@
     )]
     *picked, table, ninth, coords_near, conn_near = node_pick(*far[0:4])
     own = (table, ninth, conn_near, far[4:8])
-    halos, done = exchange(*picked, lambda held: own_gather(*own, held=held))
+    halos, done = exchange(*picked, lambda held: own_gather(*own, held=held), HOLD[0])
     first, last, oper, listed, counts, send = own_gather(*own, done=done)
     blk, *picked = make_blocks(first, last, conn_near, oper, halos, send, coords.shape[1] // LANES)
     own = (listed, counts, blk)
-    halos, done = exchange(*picked, lambda held: own_sums(*own, held=held))
+    halos, done = exchange(*picked, lambda held: own_sums(*own, held=held), HOLD[1])
     sums, weights = own_sums(*own, done=done)
     return fit(sums, weights, halos, coords_near, counts)
 

time: 25.6 us -> 25.5 us (level)
    ppermute x2, waiting for transfers between devices: 0.01 us -> 0.94 us  [exchange(): from_next = lax.ppermute(to_prev, 'dom', down)]
    ppermute x2, waiting for transfers between devices: 1.44 us -> 0.64 us  [exchange(): from_other = lax.ppermute(to_other, 'slab', swap)]
    ppermute x2, starting transfers between devices: 2.43 us -> 1.7 us  [exchange(): from_other = lax.ppermute(to_other, 'slab', swap)]
    ppermute x2, starting transfers between devices: 11 us -> 11.5 us  [exchange(): from_next = lax.ppermute(to_prev, 'dom', down)]
  transfers between devices with their start and end apart: 6 -> 6, of which waited for: 2 -> 3; matrix products, arithmetic and copies ran while one was open for 0% -> 0% of each run, Pallas kernels for 20% -> 21%
where the time goes in v5:
time: 25.5 us; the launch traced here: 25.4 us
  starting transfers between devices  15.4 us (60%)
  Pallas kernels  8.34 us (33%)
  waiting for transfers between devices  1.63 us (6%)
    ppermute x2, starting transfers between devices, exchange(): from_next = lax.ppermute(to_prev, 'dom', down)  11.5 us
    pallas_call x2, Pallas kernels, own_sums(): pl.pallas_call(late_sum_kernel if held is None else early_sum_kernel, out...  3.09 us
    ppermute x2, starting transfers between devices, exchange(): from_prev = lax.ppermute(to_next, 'dom', up)  2.2 us
    pallas_call x2, Pallas kernels, own_gather(): pl.pallas_call(late_gather_kernel if held is None else early_gather_kerne...  2.12 us
    ppermute x2, starting transfers between devices, exchange(): from_other = lax.ppermute(to_other, 'slab', swap)  1.7 us
    pallas_call x1, Pallas kernels, make_blocks(): pl.pallas_call(kernel, out_shape=(jax.ShapeDtypeStruct((64, elems), jnp.f...  1.26 us
    pallas_call x1, Pallas kernels, node_pick(): pl.pallas_call(node_pick_kernel, out_shape=(out, out, out, jax.ShapeDtype...  0.97 us
    ppermute x2, waiting for transfers between devices, exchange(): from_next = lax.ppermute(to_prev, 'dom', down)  0.94 us
  transfers between devices with their start and end apart: 6, of which 3 were waited for; matrix products, arithmetic and copies ran while one was open for 0% of the time, Pallas kernels for 21%

profile of v5, /device:TPU:1, one launch (start us, length us, event | category | flops | bytes accessed | tf_op | source)
XLA Modules:
  0.0 25.4 jit_solution(1050203935002441274)
XLA Ops:
  0.0 1.0 %node_pick.1 = (f32[9,128]{1,0:T(8,128)S(1)}, f32[9,128]{1,0:T(8,128)S(1)}, f32[9,128]{1,0:T(8,128)S(1)}, f32[11,8,128]{2,1,0:T(8,128)S(1)}, f32[16,128]{1,0:T(8...) custom-call(f32[3,1408]{1,0:T(4,128)} %coords_hbm.1, f32[6,1408]{1,0:T(8,128)} %disp_hbm.1, ...), custom_call_target="tpu_custom_call" | custom-call | tf_op jit(solution)/shard_map/node_pick/pallas_call | solution.py:94
  1.0 2.1 %collective-permute-start = (f32[9,128]{1,0:T(8,128)S(1)}, f32[9,128]{1,0:T(8,128)S(1)}, u32[]{:S(2)}, u32[]{:S(2)}) collective-permute-start(f32[9,128]{1,0:T(8,128)S(1)} %get-tuple-element.51), channel_id=1, source_target_pairs={{0,2},{2,4},{4,6},{6,8},{8,10},{10,12},{12,14},{14,16},{16,18},{18... | collective-permute-start | bytes 13832 | tf_op jit(solution)/shard_map/ppermute | solution.py:488
  3.1 2.0 %early_gather.1 = (f32[10,8,1024]{2,1,0:T(8,128)S(1)}, f32[10,1024]{1,0:T(8,128)S(1)}, bf16[30,24,1024]{2,1,0:T(8,128)(2,1)S(1)}, s32[192,128]{1,0:T(8,128)S(1)}...) custom-call(f32[11,8,128]{2,1,0:T(8,128)S(1)} %get-tuple-element.35.refs_0_, ...), custom_call_target="tpu_custom_call" | custom-call | flops 20000000 | bytes 4000000 | tf_op jit(solution)/shard_map/early_gather/pallas_call | solution.py:176
  5.1 7.2 %collective-permute-start.1 = (f32[9,128]{1,0:T(8,128)S(1)}, f32[9,128]{1,0:T(8,128)S(1)}, u32[]{:S(2)}, u32[]{:S(2)}) collective-permute-start(f32[9,128]{1,0:T(8,128)S(1)} %get-tuple-element.52), channel_id=1, source_target_pairs={{2,0},{4,2},{6,4},{8,6},{10,8},{12,10},{14,12},{16,14},{18,16},{20... | collective-permute-start | bytes 13832 | tf_op jit(solution)/shard_map/ppermute | solution.py:493
  12.3 1.0 %collective-permute-start.2 = (f32[9,128]{1,0:T(8,128)S(1)}, f32[9,128]{1,0:T(8,128)S(1)}, u32[]{:S(2)}, u32[]{:S(2)}) collective-permute-start(f32[9,128]{1,0:T(8,128)S(1)} %get-tuple-element.53), channel_id=1, source_target_pairs={{0,1},{1,0},{2,3},{3,2},{4,5},{5,4},{6,7},{7,6},{8,9},{9,8},{10,11... | collective-permute-start | bytes 13832 | tf_op jit(solution)/shard_map/ppermute | solution.py:494
  13.2 0.2 late_gather.1
  13.4 0.0 collective-permute-done.refs_4_
  13.4 0.0 collective-permute-done.1.refs_5_
  13.4 0.6 %collective-permute-done.2.refs_6_ = f32[9,128]{1,0:T(8,128)S(1)} collective-permute-done((f32[9,128]{1,0:T(8,128)S(1)}, f32[9,128]{1,0:T(8,128)S(1)}, u32[]{:S(2)}, u32[]{:S(2)}) %collective-permute-start.2) | collective-permute-done | bytes 4640 | tf_op jit(solution)/shard_map/ppermute | solution.py:494
  14.0 1.3 %make_blocks.1 = (f32[64,1024]{1,0:T(8,128)S(1)}, f32[64,128]{1,0:T(8,128)S(1)}, f32[64,128]{1,0:T(8,128)S(1)}, f32[64,128]{1,0:T(8,128)S(1)}) custom-call(f32[10,8,1024]{2,1,0:T(8,128)S(1)} %get-tuple-element.48.refs_0_, f32[10,1024]{1,0:T(8,128)S(1)} %get-tuple-element.49.refs_1_, s32[10,1024]{1,0:T(8,128)S(1)} %get-tuple-element.37.refs_2_, ...), custom_call_target="tpu_custom_call" | custom-call | tf_op jit(solution)/shard_map/make_blocks/pallas_call | solution.py:262
  15.3 0.1 collective-permute-start.3
  15.4 0.7 %collective-permute-start.5 = (f32[64,128]{1,0:T(8,128)S(1)}, f32[64,128]{1,0:T(8,128)S(1)}, u32[]{:S(2)}, u32[]{:S(2)}) collective-permute-start(f32[64,128]{1,0:T(8,128)S(1)} %get-tuple-element.63), channel_id=1, source_target_pairs={{0,1},{1,0},{2,3},{3,2},{4,5},{5,4},{6,7},{7,6},{8,9},{9,8},{10,11... | collective-permute-start | bytes 98312 | tf_op jit(solution)/shard_map/ppermute | solution.py:494
  16.1 3.1 %early_sums.1 = (f32[96,192]{1,0:T(8,128)S(1)}, bf16[384,192]{1,0:T(8,128)(2,1)S(1)}, f32[64,128]{1,0:T(8,128)S(1)}) custom-call(s32[192,128]{1,0:T(8,128)S(1)} %get-tuple-element.46.list_ref, s32[1,192]{1,0:T(1,128)S(1)} %get-tuple-element.47.count_ref, f32[64,1024]{1,0:T(8,128)S(1)} %get-tuple-element.55.blk_ref, f32[64,128]{1,0:T(8,128)S(1)} %get-tuple-element.56.refs_0_), custom_call_target="tpu_custom_call" | custom-call | flops 40000000 | bytes 8000000 | tf_op jit(solution)/shard_map/early_sums/pallas_call | solution.py:406
  19.2 4.3 %collective-permute-start.4 = (f32[64,128]{1,0:T(8,128)S(1)}, f32[64,128]{1,0:T(8,128)S(1)}, u32[]{:S(2)}, u32[]{:S(2)}) collective-permute-start(f32[64,128]{1,0:T(8,128)S(1)} %get-tuple-element.62), channel_id=1, source_target_pairs={{2,0},{4,2},{6,4},{8,6},{10,8},{12,10},{14,12},{16,14},{18,16},{20... | collective-permute-start | bytes 98312 | tf_op jit(solution)/shard_map/ppermute | solution.py:493
  23.5 0.1 collective-permute-done.3.h0_ref
  23.6 0.0 collective-permute-done.5.h2_ref
  23.6 0.9 %collective-permute-done.4.h1_ref = f32[64,128]{1,0:T(8,128)S(1)} collective-permute-done((f32[64,128]{1,0:T(8,128)S(1)}, f32[64,128]{1,0:T(8,128)S(1)}, u32[]{:S(2)}, u32[]{:S(2)}) %collective-permute-start.4) | collective-permute-done | bytes 32800 | tf_op jit(solution)/shard_map/ppermute | solution.py:493
  24.5 0.9 %fit.1 = f32[12,192]{1,0:T(8,128)} custom-call(f32[96,192]{1,0:T(8,128)S(1)} %get-tuple-element.59.sum_ref, bf16[384,192]{1,0:T(8,128)(2,1)S(1)} %get-tuple-element.60.weight_ref, f32[64,128]{1,0:T(8,128)S(1)} %collective-permute-done.3.h0_ref, f32[64,128]{1,0:T(8,128)S(1)} %collective-permute-done.4.h1_ref, f32[64,128]{1,0:T(8,128)S(1)} %collective-permute-done.5.h2_ref, ...), custom_call_target="tpu_custom_call" | custom-call | tf_op jit(solution)/shard_map/fit/pallas_call | solution.py:469
  (1 shorter events, 0.0 us)
Async XLA Ops:
  1.0 12.4 %collective-permute-start = (f32[9,128]{1,0:T(8,128)S(1)}, f32[9,128]{1,0:T(8,128)S(1)}, u32[]{:S(2)}, u32[]{:S(2)}) collective-permute-start(f32[9,128]{1,0:T(8,128)S(1)} %get-tuple-element.51), channel_id=1, source_target_pairs={{0,2},{2,4},{4,6},{6,8},{8,10},{10,12},{12,14},{14,16},{16,18},{18... | collective-permute-start | bytes 13832 | tf_op jit(solution)/shard_map/ppermute | solution.py:488
  5.1 8.3 %collective-permute-start.1 = (f32[9,128]{1,0:T(8,128)S(1)}, f32[9,128]{1,0:T(8,128)S(1)}, u32[]{:S(2)}, u32[]{:S(2)}) collective-permute-start(f32[9,128]{1,0:T(8,128)S(1)} %get-tuple-element.52), channel_id=1, source_target_pairs={{2,0},{4,2},{6,4},{8,6},{10,8},{12,10},{14,12},{16,14},{18,16},{20... | collective-permute-start | bytes 13832 | tf_op jit(solution)/shard_map/ppermute | solution.py:493
  12.3 1.8 %collective-permute-start.2 = (f32[9,128]{1,0:T(8,128)S(1)}, f32[9,128]{1,0:T(8,128)S(1)}, u32[]{:S(2)}, u32[]{:S(2)}) collective-permute-start(f32[9,128]{1,0:T(8,128)S(1)} %get-tuple-element.53), channel_id=1, source_target_pairs={{0,1},{1,0},{2,3},{3,2},{4,5},{5,4},{6,7},{7,6},{8,9},{9,8},{10,11... | collective-permute-start | bytes 13832 | tf_op jit(solution)/shard_map/ppermute | solution.py:494
  15.3 8.3 %collective-permute-start.3 = (f32[64,128]{1,0:T(8,128)S(1)}, f32[64,128]{1,0:T(8,128)S(1)}, u32[]{:S(2)}, u32[]{:S(2)}) collective-permute-start(f32[64,128]{1,0:T(8,128)S(1)} %get-tuple-element.61), channel_id=1, source_target_pairs={{0,2},{2,4},{4,6},{6,8},{8,10},{10,12},{12,14},{14,16},{16,18},{18... | collective-permute-start | bytes 98312 | tf_op jit(solution)/shard_map/ppermute | solution.py:488
  15.4 8.2 %collective-permute-start.5 = (f32[64,128]{1,0:T(8,128)S(1)}, f32[64,128]{1,0:T(8,128)S(1)}, u32[]{:S(2)}, u32[]{:S(2)}) collective-permute-start(f32[64,128]{1,0:T(8,128)S(1)} %get-tuple-element.63), channel_id=1, source_target_pairs={{0,1},{1,0},{2,3},{3,2},{4,5},{5,4},{6,7},{7,6},{8,9},{9,8},{10,11... | collective-permute-start | bytes 98312 | tf_op jit(solution)/shard_map/ppermute | solution.py:494
  19.2 5.3 %collective-permute-start.4 = (f32[64,128]{1,0:T(8,128)S(1)}, f32[64,128]{1,0:T(8,128)S(1)}, u32[]{:S(2)}, u32[]{:S(2)}) collective-permute-start(f32[64,128]{1,0:T(8,128)S(1)} %get-tuple-element.62), channel_id=1, source_target_pairs={{2,0},{4,2},{6,4},{8,6},{10,8},{12,10},{14,12},{16,14},{18,16},{20... | collective-permute-start | bytes 98312 | tf_op jit(solution)/shard_map/ppermute | solution.py:493
